TPU v7x, 32 devices: a whole 2x2x4 slice. The times are simulated.
32 devices in a mesh: rows: 8 (over z, x), keys: 4 (over y, core).
Axes of the slice: x: 2, y: 2, z: 4, core: 2. Of those that a mesh axis runs over, the one named last changes fastest.
Arguments:
- tokens: bfloat16 [8, 512, 1024], P('rows'), may hold values from -6 to 6
- cotangent: bfloat16 [8, 512, 1024], P('rows'), may hold values from -6 to 6
- segment_ids: int32 [8, 512], P('rows'), may hold values from 0 to 15, never falling along the last dimension, each value on 1 to 128 neighbouring positions
- pad_mask: int32 [8, 512], P('rows'), may hold values 0 or 1
- prefix_keys: bfloat16 [2, 64, 1024], P(None, 'keys'), may hold values from -6 to 6
- prefix_values: bfloat16 [2, 64, 1024], P(None, 'keys'), may hold values from -6 to 6
- w_query: bfloat16 [2, 1024, 1024], P(None, 'rows'), may hold values from -0.1875 to 0.1875
- w_key: bfloat16 [2, 1024, 1024], P(None, 'rows'), may hold values from -0.1875 to 0.1875
- w_value: bfloat16 [2, 1024, 1024], P(None, 'rows'), may hold values from -0.1875 to 0.1875
- w_out: bfloat16 [2, 1024, 1024], P(None, 'rows'), may hold values from -1 to 1
- w_up: bfloat16 [2, 1024, 4096], P(None, 'rows', 'keys'), may hold values from -0.1875 to 0.1875
- w_down_t: bfloat16 [2, 1024, 4096], P(None, 'rows', 'keys'), may hold values from -0.09375 to 0.09375
- norm1_gain: float32 [2, 1024], replicated, may hold values from 0.5 to 1.5
- norm1_bias: float32 [2, 1024], replicated, may hold values from -1.2 to 1.2
- norm2_gain: float32 [2, 1024], replicated, may hold values from 0.5 to 1.5
- norm2_bias: float32 [2, 1024], replicated, may hold values from -1.2 to 1.2
Outputs:
- activations: bfloat16 [8, 512, 1024], P('rows')
- grad_tokens: float32 [8, 512, 1024], P('rows')
- grad_prefix_keys: float32 [2, 64, 1024], P(None, 'keys')
- grad_prefix_values: float32 [2, 64, 1024], P(None, 'keys')
Inputs may be any that keep to these rules, and one draw needn't show every extreme that they name: `segment_ids`: in each row the ids never fall; every id of 0 to 15 covers 1 to 128 consecutive tokens, and some sentence covers exactly 128.
All inputs are finite; a program needn't handle non-finite values. No bound on the sum of `pad_mask` on one device may be relied on, other than what follows from the above.
Results may differ from a plain program's by a relative error of at most 0.03.
Values may be sent and summed in bfloat16 or wider, within the bound.
A program may use at most 192 MiB of HBM per device.

v0:
```python
import jax
import jax.numpy as jnp
from jax import lax
from jax.sharding import PartitionSpec as P

HEADS = 16
HEAD = 64
LAYERS = 2


EPSILON = 1e-05
NEGATIVE = -1000000000.0


def combined_all(value, axis, combine):
    everything = jax.tree.map(lambda part: lax.all_gather(part, axis), value)
    first = jax.tree.map(lambda part: part[0], everything)

    def hop(k, so_far):
        return combine(so_far, jax.tree.map(lambda part: part[k], everything))

    return lax.fori_loop(1, lax.axis_size(axis), hop, first)


def normalize(inputs, gain_vec, shift_vec):
    centre = inputs - jnp.mean(inputs, axis=-1, keepdims=True)
    spread = jnp.mean(centre * centre, axis=-1, keepdims=True)
    return centre * lax.rsqrt(spread + EPSILON) * gain_vec + shift_vec


def gelu_exact(inputs):
    return jax.nn.gelu(inputs, approximate=False)


def contract_last(left_side, right_side):
    return lax.dot_general(
        left_side, right_side, (((1,), (1,)), ((), ())), preferred_element_type=jnp.float32
    )


def combine_stats(earlier, later):
    maxima = jnp.maximum(earlier[0], later[0])
    totals = earlier[1] * jnp.exp(earlier[0] - maxima) + later[1] * jnp.exp(later[0] - maxima)
    return (maxima, totals)


def visibility(query_segments, key_segments, key_padding, prefix_count):
    same_segment = (query_segments[:, None] == key_segments[None, :]) & (key_padding[None, :] == 1)
    prefix_cols = jnp.ones((query_segments.shape[0], prefix_count), dtype=bool)
    return jnp.concatenate([prefix_cols, same_segment], axis=1)


def block_scores(query_block, key_heads, visible):
    scores = jnp.einsum("qhd,khd->hqk", query_block, key_heads, preferred_element_type=jnp.float32)
    return jnp.where(visible[None], scores, NEGATIVE)


def forward_layer(hidden_low, hidden, weights, norm_params, prefix_key, prefix_value, layout):
    w_query, w_key, w_value, w_out, w_up, w_down = weights
    gain_one, bias_one, gain_two, bias_two = norm_params
    segment_row, key_segments, key_padding, start_row, own_count, block_rows = layout
    prefix_count = prefix_key.shape[0]
    queries = (
        jnp.dot(hidden_low, w_query, preferred_element_type=jnp.float32) * HEAD ** (-0.5)
    ).astype(jnp.bfloat16)
    own_low = lax.dynamic_slice_in_dim(hidden_low, start_row, own_count, 0)
    keys_own = jnp.dot(own_low, w_key, preferred_element_type=jnp.float32).astype(jnp.bfloat16)
    values_own = jnp.dot(own_low, w_value, preferred_element_type=jnp.float32).astype(jnp.bfloat16)
    key_heads = jnp.concatenate([prefix_key, keys_own], axis=0).reshape(
        prefix_count + own_count, HEADS, HEAD
    )
    value_heads = jnp.concatenate([prefix_value, values_own], axis=0).reshape(
        prefix_count + own_count, HEADS, HEAD
    )
    query_block = queries.reshape(block_rows, HEADS, HEAD)
    visible = visibility(segment_row, key_segments, key_padding, prefix_count)
    scores = block_scores(query_block, key_heads, visible)
    local_max = jnp.max(scores, axis=-1)
    totals_parts = jnp.sum(jnp.exp(scores - local_max[:, :, None]), axis=-1)
    maxima, totals = combined_all((local_max, totals_parts), "keys", combine_stats)
    log_total = maxima + jnp.log(totals)
    shares = jnp.exp(scores - log_total[:, 0:block_rows, None]).astype(jnp.bfloat16)
    partials = jnp.einsum(
        "hqk,khd->qhd", shares, value_heads, preferred_element_type=jnp.float32
    ).reshape(block_rows, HEADS * HEAD)
    attended = lax.psum(partials.astype(jnp.bfloat16), "keys")
    branch = jnp.dot(attended, w_out, preferred_element_type=jnp.float32)
    middle_pre = hidden + branch
    middle = normalize(middle_pre, gain_one, bias_one)
    up_proj = jnp.dot(middle.astype(jnp.bfloat16), w_up, preferred_element_type=jnp.float32)
    activated = gelu_exact(up_proj).astype(jnp.bfloat16)
    feed_out = lax.psum(contract_last(activated, w_down).astype(jnp.bfloat16), "keys").astype(
        jnp.float32
    )
    output_pre = middle + feed_out
    output = normalize(output_pre, gain_two, bias_two)
    output_low = output.astype(jnp.bfloat16)
    return (
        output,
        output_low,
        (queries, key_heads, value_heads, log_total, middle_pre, up_proj, output_pre),
    )


def backward_layer(gradient, saved_state, weights, norm_params, layout):
    w_query, w_key, w_value, w_out, w_up, w_down = weights
    gain_one, bias_one, gain_two, bias_two = norm_params
    segment_row, key_segments, key_padding, start_row, own_count, block_rows = layout
    queries, key_heads, value_heads, log_total, middle_pre, up_proj, output_pre = saved_state
    prefix_count = key_heads.shape[0] - own_count
    _, norm_two_back = jax.vjp(lambda inputs: normalize(inputs, gain_two, bias_two), output_pre)
    (grad_output_pre,) = norm_two_back(gradient)
    grad_feed = grad_output_pre.astype(jnp.bfloat16)
    grad_activated = jnp.dot(grad_feed, w_down, preferred_element_type=jnp.float32)
    _, gelu_back = jax.vjp(gelu_exact, up_proj)
    (grad_up,) = gelu_back(grad_activated)
    grad_middle_part = contract_last(grad_up.astype(jnp.bfloat16), w_up)
    grad_middle = grad_output_pre + lax.psum(grad_middle_part.astype(jnp.bfloat16), "keys").astype(
        jnp.float32
    )
    _, norm_one_back = jax.vjp(lambda inputs: normalize(inputs, gain_one, bias_one), middle_pre)
    (grad_middle_pre,) = norm_one_back(grad_middle)
    grad_attended = contract_last(grad_middle_pre.astype(jnp.bfloat16), w_out).astype(jnp.bfloat16)
    block_index = 0
    first_row = block_index * block_rows
    query_block = queries.reshape(block_rows, HEADS, HEAD)
    grad_block = grad_attended.reshape(block_rows, HEADS, HEAD)
    visible = visibility(segment_row, key_segments, key_padding, prefix_count)
    shares = jnp.exp(
        block_scores(query_block, key_heads, visible)
        - log_total[:, first_row : first_row + block_rows, None]
    )
    grad_shares = jnp.einsum(
        "qhd,khd->hqk", grad_block, value_heads, preferred_element_type=jnp.float32
    )
    row_terms = jnp.sum(shares * grad_shares, axis=-1)
    kept_blocks = [(query_block, grad_block, shares, grad_shares)]
    row_dot = lax.psum(row_terms.astype(jnp.bfloat16), "keys").astype(jnp.float32)
    block_index = 0
    first_row = block_index * block_rows
    query_block, grad_block, shares, grad_shares = kept_blocks[block_index]
    grad_scores = (
        shares * (grad_shares - row_dot[:, first_row : first_row + block_rows, None])
    ).astype(jnp.bfloat16)
    query_parts = jnp.einsum(
        "hqk,khd->qhd", grad_scores, key_heads, preferred_element_type=jnp.float32
    ).reshape(block_rows, HEADS * HEAD)
    grad_key_heads = jnp.einsum(
        "hqk,qhd->khd", grad_scores, query_block, preferred_element_type=jnp.float32
    )
    grad_value_heads = jnp.einsum(
        "hqk,qhd->khd", shares.astype(jnp.bfloat16), grad_block, preferred_element_type=jnp.float32
    )
    grad_keys = grad_key_heads.reshape(key_heads.shape[0], HEADS * HEAD)
    grad_values = grad_value_heads.reshape(value_heads.shape[0], HEADS * HEAD)
    kv_term = contract_last(grad_keys[prefix_count:].astype(jnp.bfloat16), w_key) + contract_last(
        grad_values[prefix_count:].astype(jnp.bfloat16), w_value
    )
    query_scale = HEAD ** (-0.5)
    query_rows = lax.psum(query_parts.astype(jnp.bfloat16), "keys")
    whole_query = contract_last(query_rows, w_query) * query_scale
    gathered = lax.all_gather(kv_term.astype(jnp.bfloat16), "keys", axis=0, tiled=True).astype(
        kv_term.dtype
    )
    return (
        grad_middle_pre + gathered + whole_query,
        grad_keys[:prefix_count],
        grad_values[:prefix_count],
    )


def per_device(
    tokens,
    cotangent,
    segment_ids,
    pad_mask,
    prefix_keys,
    prefix_values,
    w_query,
    w_key,
    w_value,
    w_out,
    w_up,
    w_down_t,
    norm1_gain,
    norm1_bias,
    norm2_gain,
    norm2_bias,
):
    gathered = (
        lax.all_gather(w_query, "rows", axis=1, tiled=True),
        lax.all_gather(w_key, "rows", axis=1, tiled=True),
        lax.all_gather(w_value, "rows", axis=1, tiled=True),
        lax.all_gather(w_out, "rows", axis=1, tiled=True),
        lax.all_gather(w_up, "rows", axis=1, tiled=True),
        lax.all_gather(w_down_t, "rows", axis=1, tiled=True),
    )
    token_count = tokens.shape[1]
    own_count = token_count // lax.axis_size("keys")
    start_row = lax.axis_index("keys") * own_count
    segment_row = segment_ids[0]
    layout = (
        segment_row,
        lax.dynamic_slice_in_dim(segment_row, start_row, own_count, 0),
        lax.dynamic_slice_in_dim(pad_mask[0], start_row, own_count, 0),
        start_row,
        own_count,
        min(512, token_count),
    )
    hidden_low = tokens[0]
    hidden = tokens[0].astype(jnp.float32)
    gradient = cotangent[0].astype(jnp.float32)
    saved_layers = []
    for layer_index in range(LAYERS):
        weights = tuple((matrix[layer_index] for matrix in gathered))
        norm_params = (
            norm1_gain[layer_index],
            norm1_bias[layer_index],
            norm2_gain[layer_index],
            norm2_bias[layer_index],
        )
        hidden, hidden_low, saved_state = forward_layer(
            hidden_low,
            hidden,
            weights,
            norm_params,
            prefix_keys[layer_index],
            prefix_values[layer_index],
            layout,
        )
        saved_layers.append(saved_state)
    activations = hidden_low[None]
    back_weights = (
        lax.all_gather(w_query, "rows", axis=1, tiled=True),
        lax.all_gather(w_key, "rows", axis=1, tiled=True),
        lax.all_gather(w_value, "rows", axis=1, tiled=True),
        lax.all_gather(w_out, "rows", axis=1, tiled=True),
        lax.all_gather(w_up, "rows", axis=1, tiled=True),
        lax.all_gather(w_down_t, "rows", axis=1, tiled=True),
    )
    key_list = []
    value_list = []
    for layer_index in reversed(range(LAYERS)):
        weights = tuple((matrix[layer_index] for matrix in back_weights))
        norm_params = (
            norm1_gain[layer_index],
            norm1_bias[layer_index],
            norm2_gain[layer_index],
            norm2_bias[layer_index],
        )
        gradient, grad_key_rows, grad_value_rows = backward_layer(
            gradient, saved_layers[layer_index], weights, norm_params, layout
        )
        key_list.insert(0, grad_key_rows)
        value_list.insert(0, grad_value_rows)
    prefix_sums = lax.psum((jnp.stack(key_list), jnp.stack(value_list)), "rows")
    return (activations, gradient[None], prefix_sums[0], prefix_sums[1])


def solution(mesh):
    return jax.shard_map(
        per_device,
        mesh=mesh,
        in_specs=(
            P("rows", None, None),
            P("rows", None, None),
            P("rows", None),
            P("rows", None),
            P(None, "keys", None),
            P(None, "keys", None),
            P(None, "rows", None),
            P(None, "rows", None),
            P(None, "rows", None),
            P(None, "rows", None),
            P(None, "rows", "keys"),
            P(None, "rows", "keys"),
            P(),
            P(),
            P(),
            P(),
        ),
        out_specs=(
            P("rows", None, None),
            P("rows", None, None),
            P(None, "keys", None),
            P(None, "keys", None),
        ),
        check_vma=False,
    )
```

profile of v0, /device:TPU:1, one launch (start us, length us, event | category | flops | bytes accessed | tf_op | source)
XLA Modules:
  0.0 1044.2 jit_solution(1006538118075318613)
XLA Ops:
  11.3 73.2 %all-gather.13.cloned.1.call-done = bf16[2,1024,1024]{2,1,0:T(8,128)(2,1)} async-done(((bf16[2,128,1024]{2,1,0:T(8,128)(2,1)}), bf16[2,1024,1024]{2,1,0:T(8,128)(2,1)}) %all-gather.13.cloned.1.call-update) | async-done | bytes 4194320 | tf_op jit(solution)/shard_map/all_gather | solution.py:193
  84.5 2.0 fusion.60
  86.8 71.6 %all-gather.17.cloned.1.call-done = bf16[2,1024,1024]{2,1,0:T(8,128)(2,1)} async-done(((bf16[2,128,1024]{2,1,0:T(8,128)(2,1)}), bf16[2,1024,1024]{2,1,0:T(8,128)(2,1)}) %all-gather.17.cloned.1.call-update) | async-done | bytes 4194320 | tf_op jit(solution)/shard_map/all_gather | solution.py:192
  158.4 2.0 fusion.59
  160.6 71.6 %all-gather.15.cloned.1.call-done = bf16[2,1024,1024]{2,1,0:T(8,128)(2,1)} async-done(((bf16[2,128,1024]{2,1,0:T(8,128)(2,1)}), bf16[2,1024,1024]{2,1,0:T(8,128)(2,1)}) %all-gather.15.cloned.1.call-update) | async-done | bytes 4194320 | tf_op jit(solution)/shard_map/all_gather | solution.py:191
  232.3 3.2 multiply_convert_fusion.5
  237.5 7.1 all-gather
  245.5 5.4 all-gather.1
  251.1 4.6 convolution_convert_fusion.3
  258.0 48.0 %all-gather.19.cloned.1.call-done = bf16[2,1024,1024]{2,1,0:T(8,128)(2,1)} async-done(((bf16[2,128,1024]{2,1,0:T(8,128)(2,1)}), bf16[2,1024,1024]{2,1,0:T(8,128)(2,1)}) %all-gather.19.cloned.1.call-update) | async-done | bytes 4194320 | tf_op jit(solution)/shard_map/all_gather | solution.py:194
  306.0 38.1 %all-reduce.12.cloned.1.call-done = bf16[512,1024]{0,1:T(8,128)(2,1)} async-done(((bf16[512,1024]{0,1:T(8,128)(2,1)}), bf16[512,1024]{0,1:T(8,128)(2,1)}) %all-reduce.12.cloned.1.call-update) | async-done | bytes 1048592 | tf_op jit(solution)/shard_map/psum | solution.py:86
  344.1 3.3 fusion.140
  347.8 71.4 %all-gather.21.cloned.1.call-done = bf16[2,1024,1024]{2,1,0:T(8,128)(2,1)} async-done(((bf16[2,128,1024]{2,1,0:T(8,128)(2,1)}), bf16[2,1024,1024]{2,1,0:T(8,128)(2,1)}) %all-gather.21.cloned.1.call-update) | async-done | bytes 4194320 | tf_op jit(solution)/shard_map/all_gather | solution.py:195
  419.2 4.2 fusion.30
  423.4 69.9 %all-gather.23.cloned.1.call-done = bf16[2,1024,1024]{2,1,0:T(8,128)(2,1)} async-done(((bf16[2,128,1024]{2,1,0:T(8,128)(2,1)}), bf16[2,1024,1024]{2,1,0:T(8,128)(2,1)}) %all-gather.23.cloned.1.call-update) | async-done | bytes 4194320 | tf_op jit(solution)/shard_map/all_gather | solution.py:196
  493.3 8.3 fusion.52
  503.9 33.3 %all-reduce.14.cloned.1.call-done = bf16[512,1024]{1,0:T(8,128)(2,1)} async-done(((bf16[512,1024]{1,0:T(8,128)(2,1)}), bf16[512,1024]{1,0:T(8,128)(2,1)}) %all-reduce.14.cloned.1.call-update) | async-done | bytes 1048592 | tf_op jit(solution)/shard_map/psum | solution.py:92
  537.2 1.9 fusion.133
  540.5 1.6 copy-done.65
  543.2 1.8 copy.49
  545.0 3.8 multiply_convert_fusion.3
  550.4 2.9 fusion.58
  553.2 1.8 copy.46
  555.0 2.4 select_reduce_fusion
  557.4 6.2 all-gather.2
  564.4 5.6 all-gather.3
  570.7 2.5 while.35
  573.3 4.8 convolution_convert_fusion.2
  578.2 35.9 %all-reduce.16.cloned.1.call-done = bf16[512,1024]{0,1:T(8,128)(2,1)} async-done(((bf16[512,1024]{0,1:T(8,128)(2,1)}), bf16[512,1024]{0,1:T(8,128)(2,1)}) %all-reduce.16.cloned.1.call-update) | async-done | bytes 1048592 | tf_op jit(solution)/shard_map/psum | solution.py:86
  614.1 4.2 fusion.141
  621.7 6.3 fusion.49
  628.5 36.1 %all-reduce.18.cloned.1.call-done = bf16[512,1024]{1,0:T(8,128)(2,1)} async-done(((bf16[512,1024]{1,0:T(8,128)(2,1)}), bf16[512,1024]{1,0:T(8,128)(2,1)}) %all-reduce.18.cloned.1.call-update) | async-done | bytes 1048592 | tf_op jit(solution)/shard_map/psum | solution.py:92
  664.6 2.7 fusion.132
  668.0 2.6 fusion.131
  670.5 11.0 %fusion.50 = bf16[512,1024]{1,0:T(8,128)(2,1)} fusion(bf16[2,1024,1024]{2,1,0:T(8,128)(2,1)} %all-gather.21.cloned.1.call-done, f32[512,1024]{1,0:T(8,128)} %copy-done.72, bf16[2,1024,1024]{2,1,0:T(8,128)(2,1)} %all-gather.23.cloned.1.call-done, f32[512,1024]{1,0:T(8,128)} %get-tuple-element.309, f32[512]{0:T(512)S(1)} %negate_multiply_fusion.5), kind=kOutput, calls=%fused_computation.129 | convolution fusion | flops 2186805248 | bytes 9439232 | tf_op jit(solution)/shard_map/dot_general | solution.py:36
  681.8 36.4 %all-reduce.20.cloned.1.call-done = bf16[512,1024]{1,0:T(8,128)(2,1)} async-done(((bf16[512,1024]{1,0:T(8,128)(2,1)}), bf16[512,1024]{1,0:T(8,128)(2,1)}) %all-reduce.20.cloned.1.call-update) | async-done | bytes 1048592 | tf_op jit(solution)/shard_map/psum | solution.py:118
  718.2 3.4 multiply_reduce_fusion.4
  725.2 2.3 fusion.51
  727.5 2.3 copy.50
  729.8 4.9 convolution_bitcast_fusion.2
  734.7 6.2 multiply_reduce_fusion.1
  740.9 9.4 psum.89
  750.4 5.2 multiply_convert_fusion.1
  755.6 1.9 convolution_bitcast_fusion.3
  759.3 2.4 fusion.33
  761.8 3.1 fusion.62
  765.2 31.2 %all-reduce.22.cloned.1.call-done = bf16[512,1024]{0,1:T(8,128)(2,1)} async-done(((bf16[512,1024]{0,1:T(8,128)(2,1)}), bf16[512,1024]{0,1:T(8,128)(2,1)}) %all-reduce.22.cloned.1.call-update) | async-done | bytes 1048592 | tf_op jit(solution)/shard_map/psum | solution.py:160
  796.4 19.3 %all-gather.25.cloned.1.call-done = bf16[512,1024]{1,0:T(8,128)(2,1)} async-done(((bf16[128,1024]{1,0:T(8,128)(2,1)}), bf16[512,1024]{1,0:T(8,128)(2,1)}) %all-gather.25.cloned.1.call-update) | async-done | bytes 1048592 | tf_op jit(solution)/shard_map/all_gather | solution.py:162
  815.7 5.5 multiply_reduce_fusion.3
  821.3 1.9 fusion.129
  823.2 11.1 %fusion.53 = bf16[512,1024]{1,0:T(8,128)(2,1)} fusion(bf16[2,1024,1024]{2,1,0:T(8,128)(2,1)} %all-gather.21.cloned.1.call-done, f32[512,1024]{1,0:T(8,128)} %fusion.30, bf16[2,1024,1024]{2,1,0:T(8,128)(2,1)} %all-gather.23.cloned.1.call-done, f32[512,1024]{1,0:T(8,128)} %get-tuple-element.305, f32[512]{0:T(512)S(1)} %negate_multiply_fusion.3), kind=kOutput, calls=%fused_computation.132 | convolution fusion | flops 2186805248 | bytes 9439232 | tf_op jit(solution)/shard_map/dot_general | solution.py:36
  834.6 35.3 %all-reduce.24.cloned.1.call-done = bf16[512,1024]{1,0:T(8,128)(2,1)} async-done(((bf16[512,1024]{1,0:T(8,128)(2,1)}), bf16[512,1024]{1,0:T(8,128)(2,1)}) %all-reduce.24.cloned.1.call-update) | async-done | bytes 1048592 | tf_op jit(solution)/shard_map/psum | solution.py:118
  869.9 2.8 multiply_reduce_fusion.2
  877.8 3.5 convolution_bitcast_fusion
  881.3 6.2 multiply_reduce_fusion
  887.5 9.4 psum.92
  896.9 5.3 multiply_convert_fusion
  905.2 2.4 fusion.21
  907.6 3.2 fusion.61
  913.2 29.1 %all-reduce.26.cloned.1.call-done = bf16[512,1024]{0,1:T(8,128)(2,1)} async-done(((bf16[512,1024]{0,1:T(8,128)(2,1)}), bf16[512,1024]{0,1:T(8,128)(2,1)}) %all-reduce.26.cloned.1.call-update) | async-done | bytes 1048592 | tf_op jit(solution)/shard_map/psum | solution.py:160
  942.3 19.2 %all-gather.27.cloned.1.call-done = bf16[512,1024]{1,0:T(8,128)(2,1)} async-done(((bf16[128,1024]{1,0:T(8,128)(2,1)}), bf16[512,1024]{1,0:T(8,128)(2,1)}) %all-gather.27.cloned.1.call-update) | async-done | bytes 1048592 | tf_op jit(solution)/shard_map/all_gather | solution.py:162
  961.5 5.7 add_bitcast_fusion
  967.2 66.9 %all-reduce.28.cloned.1.call-done = (f32[2,16,1024]{2,1,0:T(8,128)}, f32[2,16,1024]{2,1,0:T(8,128)}) async-done(((f32[2,16,1024]{2,1,0:T(8,128)}, f32[2,16,1024]{2,1,0:T(8,128)}), (f32[2,16,1024]{2,1,0:T(8,128)}, f32[2,16,1024]{2,1,0:T(8,128)})) %all-reduce.28.cloned.1.call-update) | async-done | bytes 262160 | tf_op jit(solution)/shard_map/psum | solution.py:256
  1034.1 1.6 copy.84
  (260 shorter events, 42.9 us)
Async XLA Ops:
  7.2 3.1 copy-start.37
  7.2 4.0 copy-start.64
  7.2 77.3 %copy-start.70 = (bf16[1,512,1024]{2,1,0:T(8,128)(2,1)S(1)}, bf16[1,512,1024]{2,1,0:T(8,128)(2,1)}, u32[]{:S(2)}) copy-start(bf16[1,512,1024]{2,1,0:T(8,128)(2,1)} %param.20) | copy-start | bytes 3145732
  7.2 77.3 %all-gather.13.cloned.1.call-start = ((), (), s32[]{:S(2)}) async-start(), calls=%async_computation | async-start | bytes 4718592 | tf_op jit(solution)/shard_map/all_gather | solution.py:193
  7.9 150.5 %all-gather.17.cloned.1.call-start = ((), (), s32[]{:S(2)}) async-start(), calls=%async_computation.2 | async-start | bytes 4718592 | tf_op jit(solution)/shard_map/all_gather | solution.py:192
  8.7 223.6 %all-gather.15.cloned.1.call-start = ((), (), s32[]{:S(2)}) async-start(), calls=%async_computation.1 | async-start | bytes 4718592 | tf_op jit(solution)/shard_map/all_gather | solution.py:191
  9.4 296.6 %all-gather.19.cloned.1.call-start = ((), (), s32[]{:S(2)}) async-start(), calls=%async_computation.4 | async-start | bytes 4718592 | tf_op jit(solution)/shard_map/all_gather | solution.py:194
  10.0 334.1 %all-reduce.12.cloned.1.call-start = ((), (), s32[]{:S(2)}) async-start(), calls=%async_computation.3 | async-start | bytes 2097152 | tf_op jit(solution)/shard_map/psum | solution.py:86
  10.3 240.8 %copy-start.23 = (bf16[1,16,1024]{1,2,0:T(8,128)(2,1)}, bf16[1,16,1024]{1,2,0:T(8,128)(2,1)S(1)}, u32[]{:S(2)}) copy-start(bf16[1,16,1024]{1,2,0:T(8,128)(2,1)S(1)} %copy.40) | copy-start | bytes 98308
  10.5 225.5 %copy-start.16 = (bf16[1,16,1024]{1,2,0:T(8,128)(2,1)}, bf16[1,16,1024]{1,2,0:T(8,128)(2,1)S(1)}, u32[]{:S(2)}) copy-start(bf16[1,16,1024]{1,2,0:T(8,128)(2,1)S(1)} %copy.43) | copy-start | bytes 98308
  86.7 164.3 %copy-start.25 = (bf16[128,1024]{0,1:T(8,128)(2,1)}, bf16[128,1024]{0,1:T(8,128)(2,1)S(1)}, u32[]{:S(2)}) copy-start(bf16[128,1024]{0,1:T(8,128)(2,1)S(1)} %copy.41) | copy-start | bytes 786436
  160.6 75.4 %copy-start.18 = (bf16[128,1024]{0,1:T(8,128)(2,1)}, bf16[128,1024]{0,1:T(8,128)(2,1)S(1)}, u32[]{:S(2)}) copy-start(bf16[128,1024]{0,1:T(8,128)(2,1)S(1)} %copy.44) | copy-start | bytes 786436
  237.5 8.0 copy-start
  251.1 4.7 copy-start.32
  255.7 88.4 %copy-start.71 = (bf16[1,512,1024]{2,1,0:T(8,128)(2,1)S(1)}, bf16[1,512,1024]{2,1,0:T(8,128)(2,1)}, u32[]{:S(2)}) copy-start(bf16[1,512,1024]{2,1,0:T(8,128)(2,1)} %param.20) | copy-start | bytes 3145732
  255.8 163.4 %all-gather.21.cloned.1.call-start = ((), (), s32[]{:S(2)}) async-start(), calls=%async_computation.5 | async-start | bytes 4718592 | tf_op jit(solution)/shard_map/all_gather | solution.py:195
  256.4 236.9 %all-gather.23.cloned.1.call-start = ((), (), s32[]{:S(2)}) async-start(), calls=%async_computation.6 | async-start | bytes 4718592 | tf_op jit(solution)/shard_map/all_gather | solution.py:196
  257.1 280.0 %all-reduce.14.cloned.1.call-start = ((), (), s32[]{:S(2)}) async-start(), calls=%async_computation.7 | async-start | bytes 2097152 | tf_op jit(solution)/shard_map/psum | solution.py:92
  347.4 189.7 %copy-start.38 = (f32[512]{0:T(512)}, f32[512]{0:T(512)S(1)}, u32[]{:S(2)}) copy-start(f32[512]{0:T(512)S(1)} %broadcast_multiply_fusion.3) | copy-start | bytes 6148
  347.8 75.7 %copy-start.49 = (f32[512]{0:T(512)}, f32[512]{0:T(512)S(1)}, u32[]{:S(2)}) copy-start(f32[512]{0:T(512)S(1)} %multiply_reduce_fusion.8) | copy-start | bytes 6148
  347.8 189.4 %copy-start.44 = (f32[512]{0:T(512)}, f32[512]{0:T(512)S(1)}, u32[]{:S(2)}) copy-start(f32[512]{0:T(512)S(1)} %fusion.95) | copy-start | bytes 6148
  423.4 79.3 %copy-start.62 = (f32[2,1024]{1,0:T(2,128)S(1)}, f32[2,1024]{1,0:T(2,128)}, u32[]{:S(2)}) copy-start(f32[2,1024]{1,0:T(2,128)} %param.34) | copy-start | bytes 24580
  423.4 79.9 %copy-start.63 = (f32[2,1024]{1,0:T(2,128)S(1)}, f32[2,1024]{1,0:T(2,128)}, u32[]{:S(2)}) copy-start(f32[2,1024]{1,0:T(2,128)} %param.35) | copy-start | bytes 24580
  501.6 112.4 %all-reduce.16.cloned.1.call-start = ((), (), s32[]{:S(2)}) async-start(), calls=%async_computation.8 | async-start | bytes 2097152 | tf_op jit(solution)/shard_map/psum | solution.py:86
  503.3 36.2 %copy-start.53 = (f32[1,1024]{1,0:T(1,128)}, f32[1,1024]{1,0:T(1,128)S(1)}, u32[]{:S(2)}) copy-start(f32[1,1024]{1,0:T(1,128)S(1)} %get-tuple-element.320) | copy-start | bytes 12292
  503.9 35.6 %copy-start.57 = (f32[1,1024]{1,0:T(1,128)}, f32[1,1024]{1,0:T(1,128)S(1)}, u32[]{:S(2)}) copy-start(f32[1,1024]{1,0:T(1,128)S(1)} %get-tuple-element.322) | copy-start | bytes 12292
  539.1 2.9 copy-start.65
  539.5 3.8 copy-start.51
  539.5 3.7 copy-start.46
  542.1 3.0 copy-start.29
  557.4 7.0 copy-start.1
  573.2 4.9 copy-start.34
  573.3 40.8 %copy-start.42 = (f32[512]{0:T(512)S(1)}, f32[512]{0:T(512)}, u32[]{:S(2)}) copy-start(f32[512]{0:T(512)} %copy-done.41) | copy-start | bytes 6148
  573.3 40.8 %copy-start.47 = (f32[512]{0:T(512)S(1)}, f32[512]{0:T(512)}, u32[]{:S(2)}) copy-start(f32[512]{0:T(512)} %copy-done.46) | copy-start | bytes 6148
  573.3 40.8 %copy-start.54 = (f32[1,1024]{1,0:T(1,128)S(1)}, f32[1,1024]{1,0:T(1,128)}, u32[]{:S(2)}) copy-start(f32[1,1024]{1,0:T(1,128)} %copy-done.53) | copy-start | bytes 12292
  573.3 40.8 %copy-start.58 = (f32[1,1024]{1,0:T(1,128)S(1)}, f32[1,1024]{1,0:T(1,128)}, u32[]{:S(2)}) copy-start(f32[1,1024]{1,0:T(1,128)} %copy-done.57) | copy-start | bytes 12292
  578.1 86.4 %all-reduce.18.cloned.1.call-start = ((), (), s32[]{:S(2)}) async-start(), calls=%async_computation.9 | async-start | bytes 2097152 | tf_op jit(solution)/shard_map/psum | solution.py:92
  614.1 4.5 copy-start.68
  628.0 39.3 %copy-start.40 = (f32[1,1024]{1,0:T(1,128)S(1)}, f32[1,1024]{1,0:T(1,128)}, u32[]{:S(2)}) copy-start(f32[1,1024]{1,0:T(1,128)} %get-tuple-element.319) | copy-start | bytes 12292
  628.0 90.2 %all-reduce.20.cloned.1.call-start = ((), (), s32[]{:S(2)}) async-start(), calls=%async_computation.10 | async-start | bytes 2097152 | tf_op jit(solution)/shard_map/psum | solution.py:118
  681.6 114.9 %all-reduce.22.cloned.1.call-start = ((), (), s32[]{:S(2)}) async-start(), calls=%async_computation.12 | async-start | bytes 2097152 | tf_op jit(solution)/shard_map/psum | solution.py:160
  718.2 3.4 copy-start.3
  718.2 3.8 copy-start.6
  718.2 4.0 copy-start.11
  729.8 4.9 copy-start.10
  729.8 4.9 copy-start.27
  729.8 4.9 copy-start.28
  759.1 56.6 %all-gather.25.cloned.1.call-start = ((), (), s32[]{:S(2)}) async-start(), calls=%async_computation.11 | async-start | bytes 1310720 | tf_op jit(solution)/shard_map/all_gather | solution.py:162
  761.8 54.0 %copy-start.43 = (f32[512]{0:T(512)S(1)}, f32[512]{0:T(512)}, u32[]{:S(2)}) copy-start(f32[512]{0:T(512)} %copy-done.41) | copy-start | bytes 6148
  761.8 54.0 %copy-start.55 = (f32[1,1024]{1,0:T(1,128)S(1)}, f32[1,1024]{1,0:T(1,128)}, u32[]{:S(2)}) copy-start(f32[1,1024]{1,0:T(1,128)} %copy-done.53) | copy-start | bytes 12292
  764.9 56.3 %copy-start.52 = (f32[512]{0:T(512)S(1)}, f32[512]{0:T(512)}, u32[]{:S(2)}) copy-start(f32[512]{0:T(512)} %copy-done.51) | copy-start | bytes 6148
  764.9 56.3 %copy-start.48 = (f32[512]{0:T(512)S(1)}, f32[512]{0:T(512)}, u32[]{:S(2)}) copy-start(f32[512]{0:T(512)} %copy-done.46) | copy-start | bytes 6148
  765.0 105.0 %all-reduce.24.cloned.1.call-start = ((), (), s32[]{:S(2)}) async-start(), calls=%async_computation.13 | async-start | bytes 2097152 | tf_op jit(solution)/shard_map/psum | solution.py:118
  815.7 5.6 copy-start.5
  823.2 46.8 %copy-start.39 = (f32[512]{0:T(512)S(1)}, f32[512]{0:T(512)}, u32[]{:S(2)}) copy-start(f32[512]{0:T(512)} %copy-done.38) | copy-start | bytes 6148
  834.3 38.4 %copy-start.50 = (f32[512]{0:T(512)S(1)}, f32[512]{0:T(512)}, u32[]{:S(2)}) copy-start(f32[512]{0:T(512)} %copy-done.49) | copy-start | bytes 6148
  834.3 38.4 %copy-start.45 = (f32[512]{0:T(512)S(1)}, f32[512]{0:T(512)}, u32[]{:S(2)}) copy-start(f32[512]{0:T(512)} %copy-done.44) | copy-start | bytes 6148
  834.3 108.0 %all-reduce.26.cloned.1.call-start = ((), (), s32[]{:S(2)}) async-start(), calls=%async_computation.15 | async-start | bytes 2097152 | tf_op jit(solution)/shard_map/psum | solution.py:160
  877.8 3.5 copy-start.24
  877.8 3.5 copy-start.26
  896.9 5.3 copy-start.9
  905.0 56.5 %all-gather.27.cloned.1.call-start = ((), (), s32[]{:S(2)}) async-start(), calls=%async_computation.14 | async-start | bytes 1310720 | tf_op jit(solution)/shard_map/all_gather | solution.py:162
  907.6 3.3 slice-start.1
  910.8 123.3 %all-reduce.28.cloned.1.call-start = ((), (), s32[]{:S(2)}) async-start(), calls=%async_computation.16 | async-start | bytes 524288 | tf_op jit(solution)/shard_map/psum | solution.py:256
  (28 other events, 47.4 us)
Sparse Core Ops, SparseCore 0:
  10.2 74.2 all-gather.12
  86.7 71.6 all-gather.16
  160.6 71.6 all-gather.14
  234.3 71.6 all-gather.18
  308.8 35.2 all-reduce.11
  346.4 72.7 all-gather.20
  421.6 71.6 all-gather.22
  501.8 35.3 all-reduce.13
  578.3 35.7 all-reduce.15
  628.1 36.4 all-reduce.17
  681.7 36.4 all-reduce.19
  759.2 37.1 all-reduce.21
  798.0 17.7 all-gather.24
  834.4 35.4 all-reduce.23
  905.1 37.1 all-reduce.25
  943.7 17.7 all-gather.26
  965.4 68.6 all-reduce.27
where the time goes:
time: 1050 us; the launch traced here: 1040 us
  waiting for transfers between devices  791 us (75%)
  matrix products  130 us (12%)
  blocking collectives  43.2 us (4%)
  other arithmetic  35.6 us (3%)
  local copies, waits for them, and re-layouts  26.8 us (3%)
  between operations  15.4 us (1%)
    psum x2, waiting for transfers between devices, forward_layer(): attended = lax.psum(partials.astype(jnp.bfloat16), 'keys')  74 us
    all_gather x1, waiting for transfers between devices, per_device(): lax.all_gather(w_value, 'rows', axis=1, tiled=True)  73.2 us
    psum x2, waiting for transfers between devices, backward_layer(): lax.psum(grad_middle_part.astype(jnp.bfloat16), 'keys').astype(jnp.float32)  71.8 us
    all_gather x1, waiting for transfers between devices, per_device(): lax.all_gather(w_query, 'rows', axis=1, tiled=True)  71.6 us
    all_gather x1, waiting for transfers between devices, per_device(): lax.all_gather(w_key, 'rows', axis=1, tiled=True)  71.6 us
    all_gather x1, waiting for transfers between devices, per_device(): lax.all_gather(w_up, 'rows', axis=1, tiled=True)  71.4 us
    all_gather x1, waiting for transfers between devices, per_device(): lax.all_gather(w_down_t, 'rows', axis=1, tiled=True)  69.9 us
    psum x2, waiting for transfers between devices, forward_layer(): lax.psum(contract_last(activated, w_down).astype(jnp.bfloat16), 'keys')  69.4 us
  transfers between devices with their start and end apart: 17, of which 17 were waited for; matrix products, arithmetic and copies ran while one was open for 4% of the time, Pallas kernels for 0%

commit v1 on v0

v1 whole, which is shorter than its diff:
```python
import functools

import jax
import jax.numpy as jnp
from jax import lax
from jax.experimental import pallas as pl
from jax.experimental.pallas import tpu as pltpu
from jax.sharding import PartitionSpec as P

HEAD = 64
LAYERS = 2
KEYS = 4
EPSILON = 1e-05
NEGATIVE = -1000000000.0
MESH = pl.DeviceIdType.MESH
BF = jnp.bfloat16
F32 = jnp.float32

AG_M0, AG_X1, AG_M1, AG_GF1, AG_GA1, AG_GF0, AG_GA0, AG_GX, AG_ACT = range(9)
GATHERS = 9
RS_A0, RS_F0, RS_A1, RS_F1, RS_GM1, RS_GX1, RS_GM0, RS_GX0 = range(8)
SCATTERS = 8


def dot_nn(a, b):
    return lax.dot_general(a, b, (((1,), (0,)), ((), ())), preferred_element_type=F32)


def dot_nt(a, b):
    return lax.dot_general(a, b, (((1,), (1,)), ((), ())), preferred_element_type=F32)


def dot_tn(a, b):
    return lax.dot_general(a, b, (((0,), (0,)), ((), ())), preferred_element_type=F32)


def kernel(
    dims,
    tokens, cotangent, seg_row, key_code, pre_k, pre_v,
    w_query, w_key, w_value, w_out, w_up, w_down,
    g1, b1, g2, b2,
    act_out, gt_out, gpk_out, gpv_out,
    wqkv, wo, wu, wd, pk, pv,
    part, rc, ry, ys, full,
    qkv, prob, gelu_d, zhat, rinv,
    own_x, own_m, own_g, cot, att, gqkv, gk, gv, hid, go, bias,
    pg, pg_in,
    w_send, w_recv, w_fwd, loc, pre_send, pre_recv,
    rs_send, rs_recv, ag_send, ag_recv, pg_send, pg_recv, pgr_send, pgr_recv,
):
    rows, tok, width, local_ff = dims
    nz = rows // 2
    wide = width // KEYS
    heads = wide // HEAD
    own = tok // KEYS
    half = tok // 2
    depth = width // rows
    count = pre_k.shape[1]
    prefix = KEYS * count
    window = 3 * own
    col = 256

    r = lax.axis_index("rows")
    k = lax.axis_index("keys")
    z, x = r // 2, lax.rem(r, 2)
    y, c = k // 2, lax.rem(k, 2)
    sib = (r, k + 1 - 2 * c)
    across = (r, lax.rem(k + 2, KEYS))
    beside = (r + 1 - 2 * x, k)
    far, near = 1 - y, y

    def level(d):
        return lax.rem(z + d, nz)

    barrier = pltpu.get_barrier_semaphore()

    def greet(d, carry):
        pl.semaphore_signal(barrier, inc=1, device_id=(level(d) * 2 + x, k), device_id_type=MESH)
        return carry

    lax.fori_loop(1, nz, greet, 0)
    pl.semaphore_signal(barrier, inc=1, device_id=beside, device_id_type=MESH)
    for d in range(1, KEYS):
        pl.semaphore_signal(barrier, inc=1, device_id=(r, lax.rem(k + d, KEYS)), device_id_type=MESH)

    group = nz // KEYS
    first_row = k * (rows // KEYS)

    def spot(ref, layer, at):
        return ref.at[layer, pl.ds(pl.multiple_of(at * depth, depth), depth), :]

    def slot(p, zz, xx):
        layer, kind = divmod(p, 4)
        at = zz * 2 + xx
        if kind == 1:
            return spot(wo, layer, at - first_row)
        return spot((wqkv, None, wu, wd)[kind], layer, at)

    def active(p, zz):
        return None if p % 4 != 1 else (zz // group) == k

    def guarded(condition, action):
        if condition is None:
            action()
        else:
            pl.when(condition)(action)

    columns = pl.ds(pl.multiple_of(k * wide, wide), wide)

    def own_copies(p):
        layer, kind = divmod(p, 4)
        if kind == 0:
            place = pl.ds(pl.multiple_of(r * depth, depth), depth)
            return [
                pltpu.make_async_copy(
                    w.at[layer, :, columns], wqkv.at[layer, place, i * wide : (i + 1) * wide], loc.at[p, i]
                )
                for i, w in enumerate((w_query, w_key, w_value))
            ]
        source = (None, w_out, w_up, w_down)[kind]
        return [pltpu.make_async_copy(source.at[layer], slot(p, z, x), loc.at[p, 0])]

    def own_start(p):
        guarded(active(p, z), lambda: [copy.start() for copy in own_copies(p)] and None)

    def own_wait(p):
        guarded(active(p, z), lambda: [copy.wait() for copy in own_copies(p)] and None)

    def push(p, zz, xx, send_sem, target):
        place = slot(p, zz, xx)
        return pltpu.make_async_remote_copy(
            src_ref=place, dst_ref=place, send_sem=send_sem, recv_sem=w_recv.at[p, xx, zz],
            device_id=target, device_id_type=MESH,
        )

    def to_level(p, d):
        return push(p, z, x, w_send.at[p, d], (level(d) * 2 + x, k))

    def issue(p):
        def action():
            def one(d, carry):
                to_level(p, d).start()
                return carry

            lax.fori_loop(1, nz, one, 0)
            push(p, z, x, w_send.at[p, 0], beside).start()

        guarded(active(p, z), action)

    def forward(p):
        def one(d, carry):
            zz = level(d)

            def action():
                copy = push(p, zz, x, w_fwd.at[p, zz], beside)
                copy.wait_recv()
                copy.start()

            guarded(active(p, zz), action)
            return carry

        lax.fori_loop(1, nz, one, 0)

    def arrive(p):
        def one(zz, carry):
            guarded(active(p, zz), push(p, zz, 1 - x, w_fwd.at[p, zz], beside).wait_recv)
            return carry

        lax.fori_loop(0, nz, one, 0)

    def drain(p):
        def action():
            def one(d, carry):
                to_level(p, d).wait_send()
                return carry

            lax.fori_loop(1, nz, one, 0)
            push(p, z, x, w_send.at[p, 0], beside).wait_send()

        guarded(active(p, z), action)

        def passed(d, carry):
            zz = level(d)
            guarded(active(p, zz), push(p, zz, x, w_fwd.at[p, zz], beside).wait_send)
            return carry

        lax.fori_loop(1, nz, passed, 0)

    def pre_copy(i, d):
        kt = lax.rem(k + d, KEYS)
        source, target = ((pre_k, pk), (pre_v, pv))[i]
        return pltpu.make_async_remote_copy(
            src_ref=source.at[:, :, pl.ds(pl.multiple_of(kt * wide, wide), wide)],
            dst_ref=target.at[:, pl.ds(pl.multiple_of(k * count, count), count), :],
            send_sem=pre_send.at[i, d], recv_sem=pre_recv.at[i, d], device_id=(r, kt), device_id_type=MESH,
        )

    def pre_own(i):
        source, target = ((pre_k, pk), (pre_v, pv))[i]
        return pltpu.make_async_copy(
            source.at[:, :, columns],
            target.at[:, pl.ds(pl.multiple_of(k * count, count), count), :],
            pre_recv.at[i, 0],
        )

    own_block = pl.ds(pl.multiple_of(k * own, own), own)
    cot_copy = pltpu.make_async_copy(cotangent.at[own_block, :], cot, loc.at[1, 1])

    for p in range(4 * LAYERS):
        own_start(p)
    cot_copy.start()
    for i in range(2):
        pre_own(i).start()

    pl.semaphore_wait(barrier, nz - 1 + 1 + KEYS - 1)
    for p in range(4 * LAYERS):
        own_wait(p)
        issue(p)
        if p == 0:
            for i in range(2):
                for d in range(1, KEYS):
                    pre_copy(i, d).start()
    cot_copy.wait()

    def block(ref, at, *lead):
        return ref.at[(*lead, pl.ds(pl.multiple_of(at * own, own), own), slice(None))]

    def rs_copy(n, which):
        if which == 2:
            source, target, device = ys, ry.at[n], across
        else:
            at = 2 * (far, near)[which] + 1 - c
            source, target, device = block(part, at), rc.at[n, which], sib
        return pltpu.make_async_remote_copy(
            src_ref=source, dst_ref=target, send_sem=rs_send.at[n, which], recv_sem=rs_recv.at[n, which],
            device_id=device, device_id_type=MESH,
        )

    def chunks(total, body, size=16):
        def one(i, carry):
            body(pl.multiple_of(i * size, size))
            return carry

        lax.fori_loop(0, total // size, one, 0)

    def rs_far(n):
        rs_copy(n, 0).start()

    def rs_mid(n):
        rs_copy(n, 0).wait_recv()
        mine = (2 * far + c) * own

        def add(i):
            total = part[pl.ds(mine + i, 16), :].astype(F32) + rc[n, 0, pl.ds(i, 16), :].astype(F32)
            ys[pl.ds(i, 16), :] = total.astype(BF)

        chunks(own, add)
        rs_copy(n, 2).start()

    def rs_near(n):
        rs_copy(n, 1).start()

    def rs_wait(n):
        rs_copy(n, 1).wait_recv()
        rs_copy(n, 2).wait_recv()

    def rs_sum(n, i):
        mine = part[pl.ds(k * own + i, 16), :].astype(F32) + rc[n, 1, pl.ds(i, 16), :].astype(F32)
        return mine + ry[n, pl.ds(i, 16), :].astype(F32)

    def rs_end(n):
        for which in range(3):
            rs_copy(n, which).wait_send()

    def ag_copy(n, which):
        at = (k, k, lax.rem(k + 2, KEYS))[which]
        place = block(full, at, n)
        return pltpu.make_async_remote_copy(
            src_ref=place, dst_ref=place, send_sem=ag_send.at[n, which], recv_sem=ag_recv.at[n, which],
            device_id=(across, sib, sib)[which], device_id_type=MESH,
        )

    def ag_start(n):
        ag_copy(n, 0).start()
        ag_copy(n, 1).start()

    def ag_near(n):
        ag_copy(n, 1).wait_recv()

    def ag_far(n):
        ag_copy(n, 0).wait_recv()
        ag_copy(n, 2).start()
        ag_copy(n, 2).wait_recv()

    def tiles(total, body):
        def one(j, carry):
            body(pl.multiple_of(j * col, col))
            return carry

        lax.fori_loop(0, total // col, one, 0)

    def half_rows(which):
        return pl.ds(pl.multiple_of(which * half, half), half)

    def project(layer, source, which):
        hr = half_rows(which)

        def body(j):
            val = dot_nn(source[hr, :], wqkv[layer, :, pl.ds(j, col)])
            scale = jnp.where(j < wide, HEAD**-0.5, 1.0)
            qkv[layer, hr, pl.ds(j, col)] = (val * scale).astype(BF)

        tiles(3 * wide, body)

    lane_head = lax.broadcasted_iota(jnp.int32, (1, wide), 1) // HEAD
    masks = [jnp.where(lane_head == h, 1.0, 0.0).astype(BF) for h in range(heads)]

    def stacked(value):
        return jnp.concatenate([value * mask for mask in masks], axis=0)

    def place_of(i):
        return pl.multiple_of(i * own, own)

    def window_of(i):
        return pl.multiple_of(jnp.clip(i - 1, 0, KEYS - 3) * own, own)

    def unstacked(value):
        parts = [value[h * HEAD : (h + 1) * HEAD, h * own : (h + 1) * own] for h in range(heads)]
        return jnp.concatenate(parts, axis=0).T

    def attend(layer, i):
        q4 = stacked(qkv[layer, pl.ds(place_of(i), own), 0:wide])
        span = pl.ds(window_of(i), window)
        mask = bias[i]
        s_tok = dot_nt(qkv[layer, span, wide : 2 * wide], q4) + jnp.concatenate([mask] * heads, axis=1)
        s_pre = dot_nt(pk[layer], q4)
        top = jnp.maximum(jnp.max(s_tok, axis=0, keepdims=True), jnp.max(s_pre, axis=0, keepdims=True))
        e_tok, e_pre = jnp.exp(s_tok - top), jnp.exp(s_pre - top)
        inverse = 1.0 / (jnp.sum(e_tok, axis=0, keepdims=True) + jnp.sum(e_pre, axis=0, keepdims=True))
        p_tok, p_pre = e_tok * inverse, e_pre * inverse
        prob[layer, i, 0:prefix, :] = p_pre
        prob[layer, i, prefix : prefix + window, :] = p_tok
        out = dot_tn(qkv[layer, span, 2 * wide : 3 * wide], p_tok.astype(BF))
        out += dot_tn(pv[layer], p_pre.astype(BF))
        att[pl.ds(place_of(i), own), :] = unstacked(out).astype(BF)

    def attend_half(layer, which):
        def one(i, carry):
            attend(layer, 2 * which + i)
            return carry

        lax.fori_loop(0, 2, one, 0)

    def attend_back(layer, i):
        at = pl.ds(place_of(i), own)
        q4 = stacked(qkv[layer, at, 0:wide])
        go4 = stacked(go[at, :])
        start = window_of(i)
        span = pl.ds(start, window)
        p_pre = prob[layer, i, 0:prefix, :]
        p_tok = prob[layer, i, prefix : prefix + window, :]
        gp_tok = dot_nt(qkv[layer, span, 2 * wide : 3 * wide], go4)
        gp_pre = dot_nt(pv[layer], go4)
        dsum = jnp.sum(p_tok * gp_tok, axis=0, keepdims=True) + jnp.sum(p_pre * gp_pre, axis=0, keepdims=True)
        gs_tok = (p_tok * (gp_tok - dsum)).astype(BF)
        gs_pre = (p_pre * (gp_pre - dsum)).astype(BF)
        places = pl.ds(prefix + start, window)
        gk[places, :] += dot_nn(gs_tok, q4)
        gk[0:prefix, :] += dot_nn(gs_pre, q4)
        gv[places, :] += dot_nn(p_tok.astype(BF), go4)
        gv[0:prefix, :] += dot_nn(p_pre.astype(BF), go4)
        gq = dot_tn(qkv[layer, span, wide : 2 * wide], gs_tok) + dot_tn(pk[layer], gs_pre)
        gqkv[at, 0:wide] = (unstacked(gq).astype(BF).astype(F32) * HEAD**-0.5).astype(BF)

    def attend_back_half(layer, which):
        def one(i, carry):
            attend_back(layer, 2 * which + i)
            return carry

        lax.fori_loop(0, 2, one, 0)

    def out_half(layer, which):
        hr = half_rows(which)

        def body(j):
            part[hr, pl.ds(j, col)] = dot_nn(att[hr, :], wo[layer, :, pl.ds(j, col)]).astype(BF)

        tiles(width, body)

    def up_half(layer, n, which):
        hr = half_rows(which)

        def body(j):
            u = dot_nn(full[n, hr, :], wu[layer, :, pl.ds(j, col)])
            for s in range(0, half, 32):
                v = u[s : s + 32]
                phi_sum = 0.5 * (1.0 + lax.erf(v * 0.7071067811865476))
                density = jnp.exp(v * v * -0.5) * 0.3989422804014327
                at = pl.ds(pl.multiple_of(which * half, half) + s, 32)
                hid[at, pl.ds(j, col)] = (v * phi_sum).astype(BF)
                gelu_d[layer, at, pl.ds(j, col)] = phi_sum + v * density

        tiles(local_ff, body)

    def down_half(layer, which):
        hr = half_rows(which)

        def body(j):
            part[hr, pl.ds(j, col)] = dot_nt(hid[hr, :], wd[layer, pl.ds(j, col), :]).astype(BF)

        tiles(width, body)

    def down_back_half(layer, n, which):
        hr = half_rows(which)

        def body(j):
            gg = dot_nn(full[n, hr, :], wd[layer, :, pl.ds(j, col)])
            hid[hr, pl.ds(j, col)] = (gg * gelu_d[layer, hr, pl.ds(j, col)]).astype(BF)

        tiles(local_ff, body)

    def up_back_half(layer, which):
        hr = half_rows(which)

        def body(j):
            part[hr, pl.ds(j, col)] = dot_nt(hid[hr, :], wu[layer, pl.ds(j, col), :]).astype(BF)

        tiles(width, body)

    def out_back_half(layer, n, which):
        hr = half_rows(which)
        go[hr, :] = dot_nt(full[n, hr, :], wo[layer]).astype(BF)

    def project_back_half(layer, which):
        hr = half_rows(which)

        def body(j):
            part[hr, pl.ds(j, col)] = dot_nt(gqkv[hr, :], wqkv[layer, pl.ds(j, col), :]).astype(BF)

        tiles(width, body)

    def norm_into(n, residual, layer, which, gain, shift, result, target):
        index = 2 * layer + which
        g, b = gain[layer : layer + 1, :], shift[layer : layer + 1, :]

        def body(i):
            value = residual[pl.ds(i, 16), :] + rs_sum(n, i)
            centre = value - jnp.mean(value, axis=-1, keepdims=True)
            inv = lax.rsqrt(jnp.mean(centre * centre, axis=-1, keepdims=True) + EPSILON)
            hat = centre * inv
            done = hat * g + b
            zhat[index, pl.ds(i, 16), :] = hat
            rinv[index, pl.ds(i, 16), :] = inv
            result[pl.ds(i, 16), :] = done
            full[target, pl.ds(k * own + i, 16), :] = done.astype(BF)

        chunks(own, body)

    def norm_back(read, layer, which, gain, target):
        index = 2 * layer + which
        g = gain[layer : layer + 1, :]

        def body(i):
            scaled = read(i) * g
            hat = zhat[index, pl.ds(i, 16), :]
            inv = rinv[index, pl.ds(i, 16), :]
            first = jnp.mean(scaled, axis=-1, keepdims=True)
            second = jnp.mean(scaled * hat, axis=-1, keepdims=True)
            result = inv * (scaled - first - hat * second)
            own_g[pl.ds(i, 16), :] = result
            full[target, pl.ds(k * own + i, 16), :] = result.astype(BF)

        chunks(own, body)

    def mask_of(i, carry):
        queries = seg_row[:, pl.ds(place_of(i), own)]
        codes = key_code[pl.ds(window_of(i), window), :]
        bias[i] = jnp.where(codes == queries, 0.0, NEGATIVE)
        return carry

    lax.fori_loop(0, KEYS, mask_of, 0)

    def widen(i):
        own_x[pl.ds(i, 16), :] = tokens[pl.ds(k * own + i, 16), :].astype(F32)

    chunks(own, widen)

    for i in range(2):
        pre_own(i).wait()
        for d in range(1, KEYS):
            pre_copy(i, d).wait_recv()

    for layer in range(LAYERS):
        base = 4 * layer
        rs_a, rs_f = ((RS_A0, RS_F0), (RS_A1, RS_F1))[layer]
        ag_m = (AG_M0, AG_M1)[layer]
        forward(base)
        arrive(base)
        if layer == 0:
            project(layer, tokens, near)
        else:
            ag_near(AG_X1)
            project(layer, full.at[AG_X1], near)
            ag_far(AG_X1)
        project(layer, tokens if layer == 0 else full.at[AG_X1], far)
        forward(base + 1)
        attend_half(layer, far)
        arrive(base + 1)
        out_half(layer, far)
        rs_far(rs_a)
        rs_mid(rs_a)
        attend_half(layer, near)
        out_half(layer, near)
        rs_near(rs_a)
        rs_wait(rs_a)
        norm_into(rs_a, own_x, layer, 0, g1, b1, own_m, ag_m)
        ag_start(ag_m)
        rs_end(rs_a)
        forward(base + 2)
        arrive(base + 2)
        ag_near(ag_m)
        up_half(layer, ag_m, near)
        forward(base + 3)
        ag_far(ag_m)
        up_half(layer, ag_m, far)
        arrive(base + 3)
        down_half(layer, far)
        rs_far(rs_f)
        rs_mid(rs_f)
        down_half(layer, near)
        rs_near(rs_f)
        rs_wait(rs_f)
        ag_y = AG_X1 if layer == 0 else AG_ACT
        norm_into(rs_f, own_m, layer, 1, g2, b2, own_x, ag_y)
        if layer == 0:
            ag_start(ag_y)
        rs_end(rs_f)

    def prefix_copy(layer, i, d):
        kt = lax.rem(k + d, KEYS)
        source = (gk, gv)[i]
        return pltpu.make_async_remote_copy(
            src_ref=source.at[pl.ds(pl.multiple_of(kt * count, count), count), :],
            dst_ref=pg.at[layer, i, :, columns],
            send_sem=pg_send.at[layer, i, d], recv_sem=pg_recv.at[layer, i, d],
            device_id=(r, kt), device_id_type=MESH,
        )

    def prefix_own(layer, i):
        return pltpu.make_async_copy(
            (gk, gv)[i].at[pl.ds(pl.multiple_of(k * count, count), count), :],
            pg.at[layer, i, :, columns],
            pg_recv.at[layer, i, 0],
        )

    bits = rows.bit_length() - 1

    def row_copy(layer, b):
        bit = 1 << b
        partner = r + bit - 2 * bit * lax.rem(r // bit, 2)
        return pltpu.make_async_remote_copy(
            src_ref=pg.at[layer], dst_ref=pg_in.at[layer, b],
            send_sem=pgr_send.at[layer, b], recv_sem=pgr_recv.at[layer, b],
            device_id=(partner, k), device_id_type=MESH,
        )

    def row_step(layer, b):
        copy = row_copy(layer, b)
        copy.wait()
        pg[layer] += pg_in[layer, b]

    for layer in reversed(range(LAYERS)):
        rs_gm, rs_gx = ((RS_GM0, RS_GX0), (RS_GM1, RS_GX1))[layer]
        ag_gf, ag_ga = ((AG_GF0, AG_GA0), (AG_GF1, AG_GA1))[layer]
        if layer == LAYERS - 1:
            norm_back(lambda i: cot[pl.ds(i, 16), :].astype(F32), layer, 1, g2, ag_gf)
        else:
            norm_back(lambda i: own_g[pl.ds(i, 16), :] + rs_sum(RS_GX1, i), layer, 1, g2, ag_gf)
        ag_start(ag_gf)
        if layer == LAYERS - 1:
            ag_start(AG_ACT)
        else:
            rs_end(RS_GX1)
        ag_near(ag_gf)
        down_back_half(layer, ag_gf, near)
        ag_far(ag_gf)
        down_back_half(layer, ag_gf, far)
        up_back_half(layer, far)
        rs_far(rs_gm)
        rs_mid(rs_gm)
        up_back_half(layer, near)
        rs_near(rs_gm)
        rs_wait(rs_gm)
        norm_back(lambda i: own_g[pl.ds(i, 16), :] + rs_sum(rs_gm, i), layer, 0, g1, ag_ga)
        ag_start(ag_ga)
        rs_end(rs_gm)
        if layer == LAYERS - 1:
            ag_far(AG_ACT)
            ag_near(AG_ACT)
        else:
            for i in range(2):
                for d in range(1, KEYS):
                    prefix_copy(layer + 1, i, d).wait_send()
        ag_near(ag_ga)
        out_back_half(layer, ag_ga, near)
        gk[...] = jnp.zeros_like(gk)
        gv[...] = jnp.zeros_like(gv)
        attend_back_half(layer, near)
        ag_far(ag_ga)
        out_back_half(layer, ag_ga, far)
        attend_back_half(layer, far)

        def narrow(i):
            gqkv[pl.ds(i, 16), wide : 2 * wide] = gk[pl.ds(prefix + i, 16), :].astype(BF)
            gqkv[pl.ds(i, 16), 2 * wide : 3 * wide] = gv[pl.ds(prefix + i, 16), :].astype(BF)

        chunks(tok, narrow)
        project_back_half(layer, far)
        rs_far(rs_gx)
        rs_mid(rs_gx)
        for i in range(2):
            prefix_own(layer, i).start()
            for d in range(1, KEYS):
                prefix_copy(layer, i, d).start()
        project_back_half(layer, near)
        rs_near(rs_gx)
        for i in range(2):
            prefix_own(layer, i).wait()
            for d in range(1, KEYS):
                prefix_copy(layer, i, d).wait_recv()
        row_copy(layer, 0).start()
        rs_wait(rs_gx)

    act_copy = pltpu.make_async_copy(full.at[AG_ACT], act_out, loc.at[1, 2])
    act_copy.start()

    def last(i):
        full[AG_GX, pl.ds(k * own + i, 16), :] = (own_g[pl.ds(i, 16), :] + rs_sum(RS_GX0, i)).astype(BF)

    chunks(own, last)
    ag_start(AG_GX)
    rs_end(RS_GX0)
    for b in range(bits):
        for layer in range(LAYERS):
            row_step(layer, b)
            if b + 1 < bits:
                row_copy(layer, b + 1).start()
    gpk_out[...] = pg[:, 0]
    gpv_out[...] = pg[:, 1]
    for i in range(2):
        for d in range(1, KEYS):
            prefix_copy(0, i, d).wait_send()
            pre_copy(i, d).wait_send()
    for p in range(4 * LAYERS):
        drain(p)
    ag_near(AG_GX)

    def spread(which):
        def body(i):
            at = pl.ds(pl.multiple_of(which * half, half) + i, 16)
            gt_out[at, :] = full[AG_GX, at, :].astype(F32)

        chunks(half, body)

    spread(near)
    ag_far(AG_GX)
    spread(far)
    for n in range(GATHERS):
        for which in range(3):
            ag_copy(n, which).wait_send()
    act_copy.wait()


def per_device(
    tokens, cotangent, segment_ids, pad_mask, prefix_keys, prefix_values,
    w_query, w_key, w_value, w_out, w_up, w_down_t,
    norm1_gain, norm1_bias, norm2_gain, norm2_bias,
):
    rows, keys = lax.axis_size("rows"), lax.axis_size("keys")
    assert keys == KEYS and rows % (2 * KEYS) == 0 and rows & (rows - 1) == 0
    tok, width = tokens.shape[1:]
    count = prefix_keys.shape[1]
    prefix = count * keys
    local_ff = w_up.shape[2]
    wide, own, window = width // keys, tok // keys, 3 * tok // keys
    heads = wide // HEAD
    nz, bits, pieces = rows // 2, rows.bit_length() - 1, 4 * LAYERS
    seg_row = segment_ids
    key_code = jnp.where(pad_mask == 1, segment_ids, -1).reshape(tok, 1)
    vmem, anywhere = pl.BlockSpec(memory_space=pltpu.VMEM), pl.BlockSpec(memory_space=pl.ANY)
    dma = pltpu.SemaphoreType.DMA
    scratch = [
        pltpu.VMEM((LAYERS, width, 3 * wide), BF),
        pltpu.VMEM((LAYERS, wide, width), BF),
        pltpu.VMEM((LAYERS, width, local_ff), BF),
        pltpu.VMEM((LAYERS, width, local_ff), BF),
        pltpu.VMEM((LAYERS, prefix, wide), BF),
        pltpu.VMEM((LAYERS, prefix, wide), BF),
        pltpu.VMEM((tok, width), BF),
        pltpu.VMEM((SCATTERS, 2, own, width), BF),
        pltpu.VMEM((SCATTERS, own, width), BF),
        pltpu.VMEM((own, width), BF),
        pltpu.VMEM((GATHERS, tok, width), BF),
        pltpu.VMEM((LAYERS, tok, 3 * wide), BF),
        pltpu.VMEM((LAYERS, keys, prefix + window, heads * own), F32),
        pltpu.VMEM((LAYERS, tok, local_ff), F32),
        pltpu.VMEM((2 * LAYERS, own, width), F32),
        pltpu.VMEM((2 * LAYERS, own, 1), F32),
        pltpu.VMEM((own, width), F32),
        pltpu.VMEM((own, width), F32),
        pltpu.VMEM((own, width), F32),
        pltpu.VMEM((own, width), BF),
        pltpu.VMEM((tok, wide), BF),
        pltpu.VMEM((tok, 3 * wide), BF),
        pltpu.VMEM((prefix + tok, wide), F32),
        pltpu.VMEM((prefix + tok, wide), F32),
        pltpu.VMEM((tok, local_ff), BF),
        pltpu.VMEM((tok, wide), BF),
        pltpu.VMEM((keys, window, own), F32),
        pltpu.VMEM((LAYERS, 2, count, width), F32),
        pltpu.VMEM((LAYERS, bits, 2, count, width), F32),
        dma((pieces, nz)),
        dma((pieces, 2, nz)),
        dma((pieces, nz)),
        dma((pieces, 3)),
        dma((2, keys)),
        dma((2, keys)),
        dma((SCATTERS, 3)),
        dma((SCATTERS, 3)),
        dma((GATHERS, 3)),
        dma((GATHERS, 3)),
        dma((LAYERS, 2, keys)),
        dma((LAYERS, 2, keys)),
        dma((LAYERS, bits)),
        dma((LAYERS, bits)),
    ]
    act, grad, grad_keys, grad_values = pl.pallas_call(
        functools.partial(kernel, (rows, tok, width, local_ff)),
        out_shape=(
            jax.ShapeDtypeStruct((tok, width), BF),
            jax.ShapeDtypeStruct((tok, width), F32),
            jax.ShapeDtypeStruct((LAYERS, count, width), F32),
            jax.ShapeDtypeStruct((LAYERS, count, width), F32),
        ),
        in_specs=[vmem, anywhere, vmem, vmem] + [anywhere] * 8 + [vmem] * 4,
        out_specs=(anywhere, vmem, vmem, vmem),
        scratch_shapes=scratch,
        compiler_params=pltpu.CompilerParams(
            collective_id=0, has_side_effects=True, vmem_limit_bytes=62 * 1024 * 1024 - 512 * 1024
        ),
    )(
        tokens[0], cotangent[0], seg_row, key_code, prefix_keys, prefix_values,
        w_query, w_key, w_value, w_out, w_up, w_down_t,
        norm1_gain, norm1_bias, norm2_gain, norm2_bias,
    )
    return act[None], grad[None], grad_keys, grad_values


def solution(mesh):
    row3 = P("rows", None, None)
    weight = P(None, "rows", None)
    return jax.shard_map(
        per_device,
        mesh=mesh,
        in_specs=(
            row3,
            row3,
            P("rows", None),
            P("rows", None),
            P(None, "keys", None),
            P(None, "keys", None),
            weight,
            weight,
            weight,
            weight,
            P(None, "rows", "keys"),
            P(None, "rows", "keys"),
            P(),
            P(),
            P(),
            P(),
        ),
        out_specs=(row3, row3, P(None, "keys", None), P(None, "keys", None)),
        check_vma=False,
    )
```

time: 1050 us -> 350 us (0.33)
  waiting for transfers between devices: 791 us -> 0 us
  Pallas kernels: 0 us -> 340 us
  matrix products: 130 us -> 0 us
  blocking collectives: 43.2 us -> 0 us
  other arithmetic: 35.6 us -> 0.7 us
  local copies, waits for them, and re-layouts: 26.8 us -> 5.91 us
  between operations: 15.4 us -> 0.65 us
    all_gather x8 -> x0, waiting for transfers between devices: 444 us -> none  [the longest x1 73.2 us: per_device(): lax.all_gather(w_value, 'rows', axis=1, tiled=True)]
    psum x9 -> x0, waiting for transfers between devices: 342 us -> none  [the longest x2 74 us: forward_layer(): attended = lax.psum(partials.astype(jnp.bfloat16), 'keys')]
    pallas_call x0 -> x1, Pallas kernels: none -> 340 us  [per_device(): pl.pallas_call(functools.partial(kernel, (rows, tok, width, local_ff)), o...]
    dot_general x34 -> x0, matrix products: 130 us -> none  [the longest x12 62.6 us: contract_last(): lax.dot_general(left_side, right_side, (((1,), (1,)), ((), ())), preferre...]
    all_gather x4 -> x0, blocking collectives: 24.3 us -> none  [combined_all(): everything = jax.tree.map(lambda part: lax.all_gather(part, axis), value)]
    reduce_sum x14 -> x0, other arithmetic: 20.5 us -> none  [the longest x6 10.9 us: normalize(): centre = inputs - jnp.mean(inputs, axis=-1, keepdims=True)]
    psum x2 -> x0, blocking collectives: 18.9 us -> none  [backward_layer(): lax.psum(row_terms.astype(jnp.bfloat16), 'keys').astype(jnp.float32)]
    convert_element_type x5 -> x0, other arithmetic: 10.9 us -> none  [the longest x2 10.5 us: backward_layer(): grad_scores = (shares * (grad_shares - row_dot[:, first_row:first_row + b...]
  transfers between devices with their start and end apart: 17 -> 0, of which waited for: 17 -> 0; matrix products, arithmetic and copies ran while one was open for 4% -> 0% of each run, Pallas kernels for 0% -> 0%
where the time goes in v1:
time: 350 us; the launch traced here: 347 us
  Pallas kernels  340 us (97%)
  local copies, waits for them, and re-layouts  5.91 us (2%)
    pallas_call x1, Pallas kernels, per_device(): pl.pallas_call(functools.partial(kernel, (rows, tok, width, local_ff)), o...  340 us

profile of v1, /device:TPU:1, one launch (start us, length us, event | category | flops | bytes accessed | tf_op | source)
XLA Modules:
  0.0 346.9 jit_solution(14538969374790675903)
XLA Ops:
  0.6 0.7 fusion
  1.3 0.9 copy.20.key_code
  2.2 339.6 %shard_map.183 = (bf16[512,1024]{1,0:T(8,128)(2,1)}, f32[512,1024]{1,0:T(8,128)}, f32[2,16,1024]{2,1,0:T(8,128)}, f32[2,16,1024]{2,1,0:T(8,128)}) custom-call(bf16[512,1024]{1,0:T(8,128)(2,1)} %bitcast.7, bf16[512,1024]{1,0:T(8,128)(2,1)} %bitcast.8, s32[1,512]{1,0:T(1,128)} %seg_row.1, s32[512,1]{1,0:T(8,128)} %copy.20.key_code, ...), custom_call_target="tpu_custom_call" | custom-call | tf_op jit(solution)/shard_map/pallas_call | solution.py:737
  341.8 0.0 copy-start
  341.9 2.4 copy.25
  344.3 0.0 copy-done
  344.3 0.0 copy-start.2
  344.3 0.0 copy-start.1
  344.3 1.3 copy.26
  345.6 0.0 copy-done.2
  345.6 0.7 copy.27
  346.3 0.0 copy-done.1
  346.3 0.7 copy.28
Async XLA Ops:
  341.8 2.4 copy-start
  344.3 1.3 copy-start.2
  344.3 2.0 copy-start.1

commit v2 on v1

--- a/solution.py
+++ b/solution.py
@@ -45,7 +45,7 @@
     qkv, prob, gelu_d, zhat, rinv,
     own_x, own_m, own_g, cot, att, gqkv, gk, gv, hid, go, bias,
     pg, pg_in,
-    w_send, w_recv, w_fwd, loc, pre_send, pre_recv,
+    w_send, w_recv, w_over, loc, pre_send, pre_recv,
     rs_send, rs_recv, ag_send, ag_recv, pg_send, pg_recv, pgr_send, pgr_recv,
 ):
     rows, tok, width, local_ff = dims
@@ -133,58 +133,102 @@
             device_id=target, device_id_type=MESH,
         )
 
-    def to_level(p, d):
-        return push(p, z, x, w_send.at[p, d], (level(d) * 2 + x, k))
+    def straight(p):
+        return p == 4 * LAYERS - 1
+
+    def up(p, zz, xx):
+        return push(p, zz, xx, w_send.at[p, xx, zz], (lax.rem(z + 1, nz) * 2 + x, k))
+
+    def down(p, zz, xx):
+        sem = w_send.at[p, xx, jnp.where(zz == z, nz, zz)]
+        return push(p, zz, xx, sem, (lax.rem(z + nz - 1, nz) * 2 + x, k))
+
+    def over(p, zz):
+        return push(p, zz, x, w_over.at[p, zz], beside)
+
+    not_top, not_bottom = z < nz - 1, z > 0
+
+    def spread_own(p, xx, action):
+        pl.when(not_top)(lambda: action(up(p, z, xx)))
+        pl.when(not_bottom)(lambda: action(down(p, z, xx)))
+
+    def begin(copy):
+        copy.start()
+
+    def sent(copy):
+        copy.wait_send()
 
     def issue(p):
         def action():
-            def one(d, carry):
-                to_level(p, d).start()
-                return carry
-
-            lax.fori_loop(1, nz, one, 0)
-            push(p, z, x, w_send.at[p, 0], beside).start()
+            spread_own(p, x, begin)
+            over(p, z).start()
 
         guarded(active(p, z), action)
 
-    def forward(p):
-        def one(d, carry):
-            zz = level(d)
-
-            def action():
-                copy = push(p, zz, x, w_fwd.at[p, zz], beside)
-                copy.wait_recv()
-                copy.start()
-
-            guarded(active(p, zz), action)
+    def swap(p):
+        over_in = push(p, z, 1 - x, w_over.at[p, z], beside)
+        over_in.wait_recv()
+        spread_own(p, 1 - x, begin)
+
+    def hops(group, action):
+        bounds = [1 + (nz - 1) * i // 3 for i in range(4)]
+
+        def one(j, carry):
+            pl.when(z - j >= 0)(lambda: action(jnp.maximum(z - j, 0), True))
+            pl.when(z + j < nz)(lambda: action(jnp.minimum(z + j, nz - 1), False))
             return carry
 
-        lax.fori_loop(1, nz, one, 0)
+        lax.fori_loop(bounds[group], bounds[group + 1], one, 0)
+
+    def onward(p, zz, xx, below, action):
+        if below:
+            pl.when(not_top)(lambda: action(up(p, zz, xx)))
+        else:
+            pl.when(not_bottom)(lambda: action(down(p, zz, xx)))
+
+    def passes(p, group):
+        def action(zz, below):
+            def take():
+                for xx in (x, 1 - x) if straight(p) else (x,):
+                    push(p, zz, xx, w_over.at[p, zz], beside).wait_recv()
+                    onward(p, zz, xx, below, begin)
+                if not straight(p):
+                    over(p, zz).start()
+
+            guarded(active(p, zz), take)
+
+        hops(group, action)
 
     def arrive(p):
+        if straight(p):
+            return
+
         def one(zz, carry):
-            guarded(active(p, zz), push(p, zz, 1 - x, w_fwd.at[p, zz], beside).wait_recv)
+            guarded(active(p, zz), push(p, zz, 1 - x, w_over.at[p, zz], beside).wait_recv)
             return carry
 
         lax.fori_loop(0, nz, one, 0)
 
     def drain(p):
-        def action():
-            def one(d, carry):
-                to_level(p, d).wait_send()
-                return carry
-
-            lax.fori_loop(1, nz, one, 0)
-            push(p, z, x, w_send.at[p, 0], beside).wait_send()
-
-        guarded(active(p, z), action)
-
-        def passed(d, carry):
-            zz = level(d)
-            guarded(active(p, zz), push(p, zz, x, w_fwd.at[p, zz], beside).wait_send)
-            return carry
-
-        lax.fori_loop(1, nz, passed, 0)
+        def mine():
+            spread_own(p, x, sent)
+            if straight(p):
+                spread_own(p, 1 - x, sent)
+            over(p, z).wait_send()
+
+        guarded(active(p, z), mine)
+
+        def action(zz, below):
+            def passed():
+                for xx in (x, 1 - x) if straight(p) else (x,):
+                    onward(p, zz, xx, below, sent)
+                if not straight(p):
+                    over(p, zz).wait_send()
+
+            guarded(active(p, zz), passed)
+
+        for group_at in range(3):
+            hops(group_at, action)
 
     def pre_copy(i, d):
         kt = lax.rem(k + d, KEYS)
@@ -213,13 +257,15 @@
         pre_own(i).start()
 
     pl.semaphore_wait(barrier, nz - 1 + 1 + KEYS - 1)
-    for p in range(4 * LAYERS):
+    own_wait(0)
+    issue(0)
+    for i in range(2):
+        for d in range(1, KEYS):
+            pre_copy(i, d).start()
+    for p in range(1, 4 * LAYERS):
         own_wait(p)
-        issue(p)
-        if p == 0:
-            for i in range(2):
-                for d in range(1, KEYS):
-                    pre_copy(i, d).start()
+    issue(1)
+    issue(2)
     cot_copy.wait()
 
     def block(ref, at, *lead):
@@ -490,20 +536,20 @@
         for d in range(1, KEYS):
             pre_copy(i, d).wait_recv()
 
-    for layer in range(LAYERS):
+    def forward_layer(layer, first, second, third, fourth, fifth):
         base = 4 * layer
         rs_a, rs_f = ((RS_A0, RS_F0), (RS_A1, RS_F1))[layer]
         ag_m = (AG_M0, AG_M1)[layer]
-        forward(base)
+        source = tokens if layer == 0 else full.at[AG_X1]
+        first()
         arrive(base)
-        if layer == 0:
-            project(layer, tokens, near)
-        else:
+        if layer > 0:
             ag_near(AG_X1)
-            project(layer, full.at[AG_X1], near)
+        project(layer, source, near)
+        if layer > 0:
             ag_far(AG_X1)
-        project(layer, tokens if layer == 0 else full.at[AG_X1], far)
-        forward(base + 1)
+        project(layer, source, far)
+        second()
         attend_half(layer, far)
         arrive(base + 1)
         out_half(layer, far)
@@ -512,29 +558,61 @@
         attend_half(layer, near)
         out_half(layer, near)
         rs_near(rs_a)
+        third()
         rs_wait(rs_a)
         norm_into(rs_a, own_x, layer, 0, g1, b1, own_m, ag_m)
         ag_start(ag_m)
         rs_end(rs_a)
-        forward(base + 2)
+        fourth()
         arrive(base + 2)
         ag_near(ag_m)
         up_half(layer, ag_m, near)
-        forward(base + 3)
         ag_far(ag_m)
         up_half(layer, ag_m, far)
+        fifth()
         arrive(base + 3)
         down_half(layer, far)
         rs_far(rs_f)
         rs_mid(rs_f)
         down_half(layer, near)
         rs_near(rs_f)
-        rs_wait(rs_f)
-        ag_y = AG_X1 if layer == 0 else AG_ACT
-        norm_into(rs_f, own_m, layer, 1, g2, b2, own_x, ag_y)
-        if layer == 0:
-            ag_start(ag_y)
-        rs_end(rs_f)
+
+    def events(*calls):
+        def run():
+            for call in calls:
+                if len(call) == 1:
+                    issue(call[0])
+                elif call[1] == 0:
+                    swap(call[0])
+                else:
+                    passes(call[0], call[1] - 1)
+
+        return run
+
+    forward_layer(
+        0,
+        events((0, 1), (0, 2), (0, 3), (1, 1), (3,)),
+        events((1, 2), (1, 3), (2, 1)),
+        events((2, 2), (2, 3), (3, 1), (4,)),
+        events((3, 2), (3, 3), (4, 1), (5,)),
+        events((4, 2), (4, 3), (5, 1), (6,)),
+    )
+    events((5, 2), (5, 3), (6, 1), (7,))()
+    rs_wait(RS_F0)
+    norm_into(RS_F0, own_m, 0, 1, g2, b2, own_x, AG_X1)
+    ag_start(AG_X1)
+    rs_end(RS_F0)
+    forward_layer(
+        1,
+        events((6, 2), (7, 0), (6, 3)),
+        events(),
+        events((7, 1)),
+        events((7, 2)),
+        events((7, 3)),
+    )
+    rs_wait(RS_F1)
+    norm_into(RS_F1, own_m, 1, 1, g2, b2, own_x, AG_ACT)
+    rs_end(RS_F1)
 
     def prefix_copy(layer, i, d):
         kt = lax.rem(k + d, KEYS)
@@ -719,7 +797,7 @@
         pltpu.VMEM((keys, window, own), F32),
         pltpu.VMEM((LAYERS, 2, count, width), F32),
         pltpu.VMEM((LAYERS, bits, 2, count, width), F32),
-        dma((pieces, nz)),
+        dma((pieces, 2, nz + 1)),
         dma((pieces, 2, nz)),
         dma((pieces, nz)),
         dma((pieces, 3)),

time: 350 us -> 288 us (0.82)
  Pallas kernels: 340 us -> 280 us
    pallas_call x1, Pallas kernels: 340 us -> 280 us  [per_device(): pl.pallas_call(functools.partial(kernel, (rows, tok, width, local_ff)), o...]
where the time goes in v2:
time: 288 us; the launch traced here: 287 us
  Pallas kernels  280 us (97%)
  local copies, waits for them, and re-layouts  5.91 us (2%)
    pallas_call x1, Pallas kernels, per_device(): pl.pallas_call(functools.partial(kernel, (rows, tok, width, local_ff)), o...  280 us

profile of v2, /device:TPU:1, one launch (start us, length us, event | category | flops | bytes accessed | tf_op | source)
XLA Modules:
  0.0 287.4 jit_solution(8160950192805367515)
XLA Ops:
  0.6 0.7 fusion
  1.3 0.9 copy.20.key_code
  2.2 280.1 %shard_map.183 = (bf16[512,1024]{1,0:T(8,128)(2,1)}, f32[512,1024]{1,0:T(8,128)}, f32[2,16,1024]{2,1,0:T(8,128)}, f32[2,16,1024]{2,1,0:T(8,128)}) custom-call(bf16[512,1024]{1,0:T(8,128)(2,1)} %bitcast.7, bf16[512,1024]{1,0:T(8,128)(2,1)} %bitcast.8, s32[1,512]{1,0:T(1,128)} %seg_row.1, s32[512,1]{1,0:T(8,128)} %copy.20.key_code, ...), custom_call_target="tpu_custom_call" | custom-call | tf_op jit(solution)/shard_map/pallas_call | solution.py:815
  282.3 0.0 copy-start
  282.3 2.4 copy.25
  284.7 0.0 copy-done
  284.7 0.0 copy-start.2
  284.7 0.0 copy-start.1
  284.7 1.3 copy.26
  286.1 0.0 copy-done.2
  286.1 0.7 copy.27
  286.7 0.0 copy-done.1
  286.7 0.7 copy.28
Async XLA Ops:
  282.3 2.4 copy-start
  284.7 1.3 copy-start.2
  284.7 2.0 copy-start.1

commit v3 on v2

v3 whole, which is shorter than its diff:
```python
import functools

import jax
import jax.numpy as jnp
from jax import lax
from jax.experimental import pallas as pl
from jax.experimental.pallas import tpu as pltpu
from jax.sharding import PartitionSpec as P

HEAD = 64
LAYERS = 2
KEYS = 4
EPSILON = 1e-05
NEGATIVE = -1000000000.0
MESH = pl.DeviceIdType.MESH
BF = jnp.bfloat16
F32 = jnp.float32

AG_M0, AG_X1, AG_M1, AG_GF1, AG_GA1, AG_GF0, AG_GA0, AG_GX, AG_ACT = range(9)
GATHERS = 9
RS_A0, RS_F0, RS_A1, RS_F1, RS_GM1, RS_GX1, RS_GM0, RS_GX0 = range(8)
SCATTERS = 8
GATHER_BEFORE = (None, AG_M0, AG_X1, AG_M1, AG_GF1, AG_GA1, AG_GF0, AG_GA0)
SUBS = 4


def dot_nn(a, b):
    return lax.dot_general(a, b, (((1,), (0,)), ((), ())), preferred_element_type=F32)


def dot_nt(a, b):
    return lax.dot_general(a, b, (((1,), (1,)), ((), ())), preferred_element_type=F32)


def dot_tn(a, b):
    return lax.dot_general(a, b, (((0,), (0,)), ((), ())), preferred_element_type=F32)


def kernel(
    dims,
    tokens, cotangent, segments, padding, pre_k, pre_v,
    w_query, w_key, w_value, w_out, w_up, w_down,
    g1, b1, g2, b2,
    low_out, prefix_out,
    wqkv, wo, wu, wd, pk, pv,
    part, rc, ry, ys, full,
    qkv, prob, gelu_d, zhat, rinv,
    own_x, own_m, own_g, cot, att, gqkv, gk, gv, hid, go, bias, codes,
    pg, pg_low, pg_in,
    w_send, w_recv, w_over, loc, pre_send, pre_recv,
    rs_send, rs_recv, ag_send, ag_recv, pg_send, pg_recv, pgr_send, pgr_recv,
):
    rows, tok, width, local_ff = dims
    nz = rows // 2
    wide = width // KEYS
    heads = wide // HEAD
    own = tok // KEYS
    half = tok // 2
    depth = width // rows
    count = pre_k.shape[1]
    prefix = KEYS * count
    window = 3 * own

    r = lax.axis_index("rows")
    k = lax.axis_index("keys")
    z, x = r // 2, lax.rem(r, 2)
    y, c = k // 2, lax.rem(k, 2)
    sib = (r, k + 1 - 2 * c)
    across = (r, lax.rem(k + 2, KEYS))
    beside = (r + 1 - 2 * x, k)
    far, near = 1 - y, y

    def level(d):
        return lax.rem(z + d, nz)

    barrier = pltpu.get_barrier_semaphore()

    def greet(d, carry):
        pl.semaphore_signal(barrier, inc=1, device_id=(level(d) * 2 + x, k), device_id_type=MESH)
        return carry

    lax.fori_loop(1, nz, greet, 0)
    pl.semaphore_signal(barrier, inc=1, device_id=beside, device_id_type=MESH)
    for d in range(1, KEYS):
        pl.semaphore_signal(barrier, inc=1, device_id=(r, lax.rem(k + d, KEYS)), device_id_type=MESH)

    group = nz // KEYS
    first_row = k * (rows // KEYS)

    def spot(ref, layer, at):
        return ref.at[layer, pl.ds(pl.multiple_of(at * depth, depth), depth), :]

    def slot(p, zz, xx):
        layer, kind = divmod(p, 4)
        at = zz * 2 + xx
        if kind == 1:
            return spot(wo, layer, at - first_row)
        return spot((wqkv, None, wu, wd)[kind], layer, at)

    def active(p, zz):
        return None if p % 4 != 1 else (zz // group) == k

    def guarded(condition, action):
        if condition is None:
            action()
        else:
            pl.when(condition)(action)

    columns = pl.ds(pl.multiple_of(k * wide, wide), wide)

    def own_copies(p):
        layer, kind = divmod(p, 4)
        if kind == 0:
            place = pl.ds(pl.multiple_of(r * depth, depth), depth)
            return [
                pltpu.make_async_copy(
                    w.at[layer, :, columns], wqkv.at[layer, place, i * wide : (i + 1) * wide], loc.at[6 * layer + i]
                )
                for i, w in enumerate((w_query, w_key, w_value))
            ]
        source = (None, w_out, w_up, w_down)[kind]
        return [pltpu.make_async_copy(source.at[layer], slot(p, z, x), loc.at[6 * layer + 2 + kind])]

    def own_start(p):
        guarded(active(p, z), lambda: [copy.start() for copy in own_copies(p)] and None)

    def own_wait(p):
        guarded(active(p, z), lambda: [copy.wait() for copy in own_copies(p)] and None)

    def push(p, zz, xx, send_sem, target):
        place = slot(p, zz, xx)
        return pltpu.make_async_remote_copy(
            src_ref=place, dst_ref=place, send_sem=send_sem, recv_sem=w_recv.at[p, xx, zz],
            device_id=target, device_id_type=MESH,
        )

    def straight(p):
        return p == 4 * LAYERS - 1

    def up(p, zz, xx):
        return push(p, zz, xx, w_send.at[p, xx, zz], (lax.rem(z + 1, nz) * 2 + x, k))

    def down(p, zz, xx):
        sem = w_send.at[p, xx, jnp.where(zz == z, nz, zz)]
        return push(p, zz, xx, sem, (lax.rem(z + nz - 1, nz) * 2 + x, k))

    def over(p, zz):
        return push(p, zz, x, w_over.at[p, zz], beside)

    not_top, not_bottom = z < nz - 1, z > 0

    def spread_own(p, xx, action):
        pl.when(not_top)(lambda: action(up(p, z, xx)))
        pl.when(not_bottom)(lambda: action(down(p, z, xx)))

    def begin(copy):
        copy.start()

    def sent(copy):
        copy.wait_send()

    def issue(p):
        guarded(active(p, z), lambda: spread_own(p, x, begin))

    def beside_own(p):
        guarded(active(p, z), lambda: over(p, z).start())

    def swap(p):
        over_in = push(p, z, 1 - x, w_over.at[p, z], beside)
        over_in.wait_recv()
        spread_own(p, 1 - x, begin)

    def hops(group, action, sides=(True, False)):
        bounds = [1 + (nz - 1) * i // 3 for i in range(4)]

        def one(j, carry):
            if True in sides:
                pl.when(z - j >= 0)(lambda: action(jnp.maximum(z - j, 0), True))
            if False in sides:
                pl.when(z + j < nz)(lambda: action(jnp.minimum(z + j, nz - 1), False))
            return carry

        lax.fori_loop(bounds[group], bounds[group + 1], one, 0)

    def onward(p, zz, xx, below, action):
        if below:
            pl.when(not_top)(lambda: action(up(p, zz, xx)))
        else:
            pl.when(not_bottom)(lambda: action(down(p, zz, xx)))

    def passes(p, group, sides):
        def action(zz, below):
            def take():
                for xx in (x, 1 - x) if straight(p) else (x,):
                    push(p, zz, xx, w_over.at[p, zz], beside).wait_recv()
                    onward(p, zz, xx, below, begin)
                if not straight(p):
                    over(p, zz).start()

            guarded(active(p, zz), take)

        hops(group, action, sides)

    def arrive(p):
        if straight(p):
            return

        def one(zz, carry):
            guarded(active(p, zz), push(p, zz, 1 - x, w_over.at[p, zz], beside).wait_recv)
            return carry

        lax.fori_loop(0, nz, one, 0)

    def drain(p):
        def mine():
            spread_own(p, x, sent)
            if straight(p):
                spread_own(p, 1 - x, sent)
            over(p, z).wait_send()

        guarded(active(p, z), mine)

        def action(zz, below):
            def passed():
                for xx in (x, 1 - x) if straight(p) else (x,):
                    onward(p, zz, xx, below, sent)
                if not straight(p):
                    over(p, zz).wait_send()

            guarded(active(p, zz), passed)

        for group_at in range(3):
            hops(group_at, action)

    def pre_copy(i, d):
        kt = lax.rem(k + d, KEYS)
        source, target = ((pre_k, pk), (pre_v, pv))[i]
        return pltpu.make_async_remote_copy(
            src_ref=source.at[:, :, pl.ds(pl.multiple_of(kt * wide, wide), wide)],
            dst_ref=target.at[:, pl.ds(pl.multiple_of(k * count, count), count), :],
            send_sem=pre_send.at[i, d], recv_sem=pre_recv.at[i, d], device_id=(r, kt), device_id_type=MESH,
        )

    def pre_own(i):
        source, target = ((pre_k, pk), (pre_v, pv))[i]
        return pltpu.make_async_copy(
            source.at[:, :, columns],
            target.at[:, pl.ds(pl.multiple_of(k * count, count), count), :],
            pre_recv.at[i, 0],
        )

    own_block = pl.ds(pl.multiple_of(k * own, own), own)
    cot_copy = pltpu.make_async_copy(cotangent.at[own_block, :], cot, loc.at[12])

    for p in range(4 * LAYERS):
        own_start(p)
    cot_copy.start()
    for i in range(2):
        pre_own(i).start()

    visible_code = jnp.where(padding[...] == 1, segments[...], -1).astype(F32)
    codes[...] = jnp.broadcast_to(visible_code, (own, tok)).T

    def mask_of(i, carry):
        queries = segments[:, pl.ds(pl.multiple_of(i * own, own), own)].astype(F32)
        keys_code = codes[pl.ds(pl.multiple_of(jnp.clip(i - 1, 0, KEYS - 3) * own, own), window), :]
        bias[i] = jnp.where(keys_code == queries, 0.0, NEGATIVE)
        return carry

    lax.fori_loop(0, KEYS, mask_of, 0)

    def widen(i, carry):
        at = pl.multiple_of(i * 16, 16)
        own_x[pl.ds(at, 16), :] = tokens[pl.ds(k * own + at, 16), :].astype(F32)
        return carry

    lax.fori_loop(0, own // 16, widen, 0)
    pl.semaphore_wait(barrier, nz - 1 + 1 + KEYS - 1)
    own_wait(0)
    issue(0)
    beside_own(0)
    for i in range(2):
        for d in range(1, KEYS):
            pre_copy(i, d).start()
    for p in range(1, 4 * LAYERS):
        own_wait(p)
    cot_copy.wait()

    sub = own // SUBS
    block_a, block_b = 2 * far + c, 2 * far + 1 - c

    def rows_at(at, size):
        return pl.ds(pl.multiple_of(at, 16), size)

    def rs_copy(n, i):
        if i < SUBS:
            source, target = part.at[rows_at(block_b * own + i * sub, sub), :], rc.at[n, 0, i * sub : (i + 1) * sub, :]
        elif i == SUBS:
            source, target = part.at[rows_at((2 * near + 1 - c) * own, own), :], rc.at[n, 1]
        else:
            at = slice((i - SUBS - 1) * sub, (i - SUBS) * sub)
            source, target = ys.at[at, :], ry.at[n, at, :]
        return pltpu.make_async_remote_copy(
            src_ref=source, dst_ref=target, send_sem=rs_send.at[i], recv_sem=rs_recv.at[i],
            device_id=sib if i <= SUBS else across, device_id_type=MESH,
        )

    def chunks(total, body, size=16):
        def one(i, carry):
            body(pl.multiple_of(i * size, size))
            return carry

        lax.fori_loop(0, total // size, one, 0)

    def rs_mid(n, i):
        rs_copy(n, i).wait_recv()
        for at in range(i * sub, (i + 1) * sub, 16):
            mine = part[rows_at(block_a * own + at, 16), :].astype(F32)
            ys[at : at + 16, :] = (mine + rc[n, 0, at : at + 16, :].astype(F32)).astype(BF)
        rs_copy(n, SUBS + 1 + i).start()

    def rs_near(n):
        rs_copy(n, SUBS).start()

    def rs_sum(n, at):
        mine = part[rows_at(k * own + at, 16), :].astype(F32) + rc[n, 1, at : at + 16, :].astype(F32)
        return mine + ry[n, at : at + 16, :].astype(F32)

    def rs_each(n, body, target):
        if n > 0:
            ag_end(GATHER_BEFORE[n])
        rs_copy(n, SUBS).wait_recv()
        for i in range(SUBS):
            rs_copy(n, SUBS + 1 + i).wait_recv()
            for at in range(i * sub, (i + 1) * sub, 16):
                body(at)
            ag_copy(target, i).start()
        ag_copy(target, SUBS).start()
        rs_end(n)

    def rs_end(n):
        for i in range(2 * SUBS + 1):
            rs_copy(n, i).wait_send()

    def ag_copy(n, i):
        if i < SUBS:
            place, device = full.at[n, rows_at(k * own + i * sub, sub), :], across
        elif i == SUBS:
            place, device = full.at[n, rows_at(k * own, own), :], sib
        else:
            place, device = full.at[n, rows_at(block_a * own + (i - SUBS - 1) * sub, sub), :], sib
        return pltpu.make_async_remote_copy(
            src_ref=place, dst_ref=place, send_sem=ag_send.at[n // AG_ACT, i], recv_sem=ag_recv.at[n // AG_ACT, i],
            device_id=device, device_id_type=MESH,
        )

    def ag_end(n):
        for i in range(2 * SUBS + 1):
            ag_copy(n, i).wait_send()

    def ag_near(n):
        ag_copy(n, SUBS).wait_recv()

    def ag_pass(n, i):
        ag_copy(n, i).wait_recv()
        ag_copy(n, SUBS + 1 + i).start()

    def ag_got(n, i):
        ag_copy(n, SUBS + 1 + i).wait_recv()

    def ag_far(n):
        for i in range(SUBS):
            ag_pass(n, i)
        for i in range(SUBS):
            ag_got(n, i)

    def half_rows(which):
        return pl.ds(pl.multiple_of(which * half, half), half)

    def far_rows(i):
        return rows_at(block_a * own + i * sub, sub), rows_at(block_b * own + i * sub, sub)

    def both(ref, *lead, at):
        return jnp.concatenate([ref[(*lead, rows, slice(None))] for rows in at], axis=0)

    def project(layer, source, which):
        hr = half_rows(which)
        xin = source[hr, :]
        for i in range(3):
            at = slice(i * wide, (i + 1) * wide)
            val = dot_nn(xin, wqkv[layer, :, at])
            qkv[layer, hr, at] = (val * HEAD**-0.5 if i == 0 else val).astype(BF)

    lane_head = lax.broadcasted_iota(jnp.int32, (1, wide), 1) // HEAD
    masks = [jnp.where(lane_head == h, 1.0, 0.0).astype(BF) for h in range(heads)]

    def stacked(value):
        return jnp.concatenate([value * mask for mask in masks], axis=0)

    def place_of(i):
        return pl.multiple_of(i * own, own)

    def window_of(i):
        return pl.multiple_of(jnp.clip(i - 1, 0, KEYS - 3) * own, own)

    def unstacked(value):
        parts = [value[h * HEAD : (h + 1) * HEAD, h * own : (h + 1) * own] for h in range(heads)]
        return jnp.concatenate(parts, axis=0).T

    def attend(layer, i):
        q4 = stacked(qkv[layer, pl.ds(place_of(i), own), 0:wide])
        span = pl.ds(window_of(i), window)
        mask = bias[i]
        s_tok = dot_nt(qkv[layer, span, wide : 2 * wide], q4) + jnp.concatenate([mask] * heads, axis=1)
        s_pre = dot_nt(pk[layer], q4)
        top = jnp.maximum(jnp.max(s_tok, axis=0, keepdims=True), jnp.max(s_pre, axis=0, keepdims=True))
        e_tok, e_pre = jnp.exp(s_tok - top), jnp.exp(s_pre - top)
        inverse = 1.0 / (jnp.sum(e_tok, axis=0, keepdims=True) + jnp.sum(e_pre, axis=0, keepdims=True))
        p_tok, p_pre = e_tok * inverse, e_pre * inverse
        prob[layer, i, 0:prefix, :] = p_pre
        prob[layer, i, prefix : prefix + window, :] = p_tok
        out = dot_tn(qkv[layer, span, 2 * wide : 3 * wide], p_tok.astype(BF))
        out += dot_tn(pv[layer], p_pre.astype(BF))
        att[pl.ds(place_of(i), own), :] = unstacked(out).astype(BF)

    def attend_back(layer, i):
        at = pl.ds(place_of(i), own)
        q4 = stacked(qkv[layer, at, 0:wide])
        go4 = stacked(go[at, :])
        start = window_of(i)
        span = pl.ds(start, window)
        p_pre = prob[layer, i, 0:prefix, :]
        p_tok = prob[layer, i, prefix : prefix + window, :]
        gp_tok = dot_nt(qkv[layer, span, 2 * wide : 3 * wide], go4)
        gp_pre = dot_nt(pv[layer], go4)
        dsum = jnp.sum(p_tok * gp_tok, axis=0, keepdims=True) + jnp.sum(p_pre * gp_pre, axis=0, keepdims=True)
        gs_tok = (p_tok * (gp_tok - dsum)).astype(BF)
        gs_pre = (p_pre * (gp_pre - dsum)).astype(BF)
        places = pl.ds(prefix + start, window)
        gk[places, :] += dot_nn(gs_tok, q4)
        gk[0:prefix, :] += dot_nn(gs_pre, q4)
        gv[places, :] += dot_nn(p_tok.astype(BF), go4)
        gv[0:prefix, :] += dot_nn(p_pre.astype(BF), go4)
        gq = dot_tn(qkv[layer, span, wide : 2 * wide], gs_tok) + dot_tn(pk[layer], gs_pre)
        gqkv[at, 0:wide] = (unstacked(gq).astype(BF).astype(F32) * HEAD**-0.5).astype(BF)

    def two(body, which):
        def one(i, carry):
            body(2 * which + i)
            return carry

        lax.fori_loop(0, 2, one, 0)

    def out_rows(layer, at, size):
        rows_here = rows_at(at, size)
        part[rows_here, :] = dot_nn(att[rows_here, :], wo[layer]).astype(BF)

    def up_half(layer, n, which):
        hr = half_rows(which)
        u = dot_nn(full[n, hr, :], wu[layer])
        for at in range(0, half, 16):
            v = u[at : at + 16]
            phi_sum = 0.5 * (1.0 + lax.erf(v * 0.7071067811865476))
            density = jnp.exp(v * v * -0.5) * 0.3989422804014327
            here = rows_at(which * half + at, 16)
            hid[here, :] = (v * phi_sum).astype(BF)
            gelu_d[layer, here, :] = phi_sum + v * density

    def ff_back(layer, gradient, slope):
        gu = (dot_nn(gradient, wd[layer]) * slope).astype(BF)
        return dot_nt(gu, wu[layer]).astype(BF)

    def scatter_far(n, step):
        for i in range(SUBS):
            value = step(i)
            at_a, at_b = far_rows(i)
            part[at_b, :] = value[sub:]
            rs_copy(n, i).start()
            part[at_a, :] = value[:sub]
            if i > 0:
                rs_mid(n, i - 1)
        rs_mid(n, SUBS - 1)

    def project_back(layer, at, size):
        rows_here = rows_at(at, size)
        part[rows_here, :] = dot_nt(gqkv[rows_here, :], wqkv[layer]).astype(BF)

    def norm_into(n, residual, layer, which, gain, shift, result, target):
        index = 2 * layer + which
        g, b = gain[layer : layer + 1, :], shift[layer : layer + 1, :]

        def body(i):
            value = residual[i : i + 16, :] + rs_sum(n, i)
            centre = value - jnp.mean(value, axis=-1, keepdims=True)
            inv = lax.rsqrt(jnp.mean(centre * centre, axis=-1, keepdims=True) + EPSILON)
            hat = centre * inv
            done = hat * g + b
            zhat[index, i : i + 16, :] = hat
            rinv[index, i : i + 16, :] = inv
            result[i : i + 16, :] = done
            full[target, rows_at(k * own + i, 16), :] = done.astype(BF)

        return body

    def norm_back(read, layer, which, gain, target):
        index = 2 * layer + which
        g = gain[layer : layer + 1, :]

        def body(i):
            scaled = read(i) * g
            hat = zhat[index, i : i + 16, :]
            inv = rinv[index, i : i + 16, :]
            first = jnp.mean(scaled, axis=-1, keepdims=True)
            second = jnp.mean(scaled * hat, axis=-1, keepdims=True)
            result = inv * (scaled - first - hat * second)
            own_g[i : i + 16, :] = result
            full[target, rows_at(k * own + i, 16), :] = result.astype(BF)

        return body

    for i in range(2):
        pre_own(i).wait()
        for d in range(1, KEYS):
            pre_copy(i, d).wait_recv()

    def forward_layer(layer, first, second, third, fourth, fifth):
        base = 4 * layer
        rs_a, rs_f = ((RS_A0, RS_F0), (RS_A1, RS_F1))[layer]
        ag_m = (AG_M0, AG_M1)[layer]
        source = tokens if layer == 0 else full.at[AG_X1]
        first()
        arrive(base)
        if layer > 0:
            ag_near(AG_X1)
        project(layer, source, near)
        if layer > 0:
            ag_far(AG_X1)
        project(layer, source, far)
        second()
        attend(layer, block_b)
        arrive(base + 1)
        out_rows(layer, block_b * own, own)
        for i in range(SUBS):
            rs_copy(rs_a, i).start()
        attend(layer, block_a)
        out_rows(layer, block_a * own, own)
        for i in range(SUBS):
            rs_mid(rs_a, i)
        two(functools.partial(attend, layer), near)
        out_rows(layer, near * half, half)
        rs_near(rs_a)
        third()
        rs_each(rs_a, norm_into(rs_a, own_x, layer, 0, g1, b1, own_m, ag_m), ag_m)
        fourth()
        arrive(base + 2)
        ag_near(ag_m)
        up_half(layer, ag_m, near)
        ag_far(ag_m)
        up_half(layer, ag_m, far)
        fifth()
        arrive(base + 3)
        scatter_far(rs_f, lambda i: dot_nt(both(hid, at=far_rows(i)), wd[layer]).astype(BF))
        part[half_rows(near), :] = dot_nt(hid[half_rows(near), :], wd[layer]).astype(BF)
        rs_near(rs_f)

    def events(*calls):
        def run():
            for call in calls:
                if len(call) == 1:
                    issue(call[0])
                    beside_own(call[0])
                elif call[1] == 0:
                    swap(call[0])
                else:
                    passes(call[0], call[1] - 1, (True, False))

        return run

    events((1,), (2,))()
    forward_layer(
        0,
        events((0, 1), (0, 2), (0, 3), (1, 1), (3,)),
        events((1, 2), (1, 3), (2, 1)),
        events((2, 2), (2, 3), (3, 1), (4,)),
        events((3, 2), (3, 3), (4, 1), (5,)),
        events((4, 2), (4, 3), (5, 1), (6,)),
    )
    events((5, 2), (5, 3), (6, 1), (7,))()
    rs_each(RS_F0, norm_into(RS_F0, own_m, 0, 1, g2, b2, own_x, AG_X1), AG_X1)
    forward_layer(
        1,
        events((6, 2), (7, 0), (6, 3)),
        events(),
        events((7, 1)),
        events((7, 2)),
        events((7, 3)),
    )

    def prefix_copy(layer, i, d):
        kt = lax.rem(k + d, KEYS)
        source = (gk, gv)[i]
        return pltpu.make_async_remote_copy(
            src_ref=source.at[pl.ds(pl.multiple_of(kt * count, count), count), :],
            dst_ref=pg.at[layer, i, :, columns],
            send_sem=pg_send.at[i, d], recv_sem=pg_recv.at[i, d],
            device_id=(r, kt), device_id_type=MESH,
        )

    def prefix_own(layer, i):
        return pltpu.make_async_copy(
            (gk, gv)[i].at[pl.ds(pl.multiple_of(k * count, count), count), :],
            pg.at[layer, i, :, columns],
            pg_recv.at[i, 0],
        )

    bits = rows.bit_length() - 1

    def row_copy(layer, b):
        bit = 1 << b
        partner = r + bit - 2 * bit * lax.rem(r // bit, 2)
        return pltpu.make_async_remote_copy(
            src_ref=pg_low.at[layer], dst_ref=pg_in.at[layer, b],
            send_sem=pgr_send.at[layer, b], recv_sem=pgr_recv.at[layer, b],
            device_id=(partner, k), device_id_type=MESH,
        )

    def row_start(layer, b):
        low = pg[layer].astype(BF)
        pg_low[layer] = low
        pg[layer] = low.astype(F32)
        row_copy(layer, b).start()

    def row_step(layer, b):
        row_copy(layer, b).wait()
        pg[layer] += pg_in[layer, b].astype(F32)
        if b + 1 < bits:
            row_start(layer, b + 1)

    def prefix_start(layer):
        for i in range(2):
            prefix_own(layer, i).start()
            for d in range(1, KEYS):
                prefix_copy(layer, i, d).start()

    def prefix_take(layer):
        for i in range(2):
            prefix_own(layer, i).wait()
            for d in range(1, KEYS):
                prefix_copy(layer, i, d).wait_recv()
        row_start(layer, 0)

    def prefix_sent(layer):
        for i in range(2):
            for d in range(1, KEYS):
                prefix_copy(layer, i, d).wait_send()

    for layer in reversed(range(LAYERS)):
        rs_gm, rs_gx = ((RS_GM0, RS_GX0), (RS_GM1, RS_GX1))[layer]
        ag_gf, ag_ga = ((AG_GF0, AG_GA0), (AG_GF1, AG_GA1))[layer]
        if layer == LAYERS - 1:
            forth = norm_into(RS_F1, own_m, 1, 1, g2, b2, own_x, AG_ACT)
            back = norm_back(lambda i: cot[i : i + 16, :].astype(F32), layer, 1, g2, ag_gf)

            def turn(i):
                forth(i)
                back(i)

            rs_each(RS_F1, turn, ag_gf)
        else:
            rs_each(RS_GX1, norm_back(lambda i: own_g[i : i + 16, :] + rs_sum(RS_GX1, i), layer, 1, g2, ag_gf), ag_gf)
            prefix_take(layer + 1)
        ag_near(ag_gf)
        part[half_rows(near), :] = ff_back(layer, full[ag_gf, half_rows(near), :], gelu_d[layer, half_rows(near), :])
        rs_near(rs_gm)

        def step(i):
            ag_pass(ag_gf, i)
            ag_got(ag_gf, i)
            at = far_rows(i)
            return ff_back(layer, both(full, ag_gf, at=at), both(gelu_d, layer, at=at))

        scatter_far(rs_gm, step)
        if layer == 0:
            row_step(1, 0)
        gk[...] = jnp.zeros_like(gk)
        gv[...] = jnp.zeros_like(gv)
        rs_each(rs_gm, norm_back(lambda i: own_g[i : i + 16, :] + rs_sum(rs_gm, i), layer, 0, g1, ag_ga), ag_ga)
        if layer == LAYERS - 1:
            for i in range(SUBS + 1):
                ag_copy(AG_ACT, i).start()
        ag_near(ag_ga)
        go[half_rows(near), :] = dot_nt(full[ag_ga, half_rows(near), :], wo[layer]).astype(BF)
        two(functools.partial(attend_back, layer), near)
        if layer == 0:
            row_step(1, 1)
        ag_far(ag_ga)
        go[half_rows(far), :] = dot_nt(full[ag_ga, half_rows(far), :], wo[layer]).astype(BF)
        two(functools.partial(attend_back, layer), far)
        prefix_start(layer)

        def narrow(which):
            def body(i):
                i = which * half + i
                gqkv[rows_at(i, 16), wide : 2 * wide] = gk[rows_at(prefix + i, 16), :].astype(BF)
                gqkv[rows_at(i, 16), 2 * wide : 3 * wide] = gv[rows_at(prefix + i, 16), :].astype(BF)

            chunks(half, body)

        narrow(far)
        project_back(layer, block_b * own, own)
        for i in range(SUBS):
            rs_copy(rs_gx, i).start()
        project_back(layer, block_a * own, own)
        for i in range(SUBS):
            rs_mid(rs_gx, i)
        narrow(near)
        project_back(layer, near * half, half)
        rs_near(rs_gx)
        if layer == LAYERS - 1:
            ag_far(AG_ACT)
            ag_near(AG_ACT)
        else:
            for b in range(2, bits):
                row_step(1, b)
            prefix_take(0)
        prefix_sent(layer)

    act_copy = pltpu.make_async_copy(full.at[AG_ACT], low_out.at[1], loc.at[13])
    act_copy.start()

    def last(i):
        full[AG_GX, rows_at(k * own + i, 16), :] = (own_g[i : i + 16, :] + rs_sum(RS_GX0, i)).astype(BF)

    rs_each(RS_GX0, last, AG_GX)
    for p in range(4 * LAYERS):
        drain(p)
    for i in range(2):
        for d in range(1, KEYS):
            pre_copy(i, d).wait_send()
    row_step(0, 0)
    ag_near(AG_GX)

    def grad_copy(which):
        return pltpu.make_async_copy(
            full.at[AG_GX, half_rows(which), :], low_out.at[0, half_rows(which), :], loc.at[14 + (which is far)]
        )

    grad_copy(near).start()
    ag_far(AG_GX)
    grad_copy(far).start()
    for b in range(1, bits):
        row_step(0, b)
    for i in range(2):
        for layer in range(LAYERS):
            prefix_out[i, layer] = pg[layer, i]
    ag_end(AG_GX)
    ag_end(AG_ACT)
    act_copy.wait()
    grad_copy(near).wait()
    grad_copy(far).wait()


def results(low, grads, act, gt, gpk, gpv, narrow, broad, act_held, grads_held, sems):
    parts, size = narrow.shape[:2]

    def taken(i):
        return pltpu.make_async_copy(low.at[0, i * size : (i + 1) * size, :], narrow.at[i], sems.at[0, i])

    def given(i):
        return pltpu.make_async_copy(broad.at[i], gt.at[0, i * size : (i + 1) * size, :], sems.at[1, i])

    in_act = pltpu.make_async_copy(low.at[1], act_held, sems.at[2, 0])
    out_act = pltpu.make_async_copy(act_held, act.at[0], sems.at[2, 0])
    in_grads = pltpu.make_async_copy(grads, grads_held, sems.at[2, 1])
    out_grads = [pltpu.make_async_copy(grads_held.at[i], (gpk, gpv)[i], sems.at[2, 2 + i]) for i in range(2)]
    for i in range(parts):
        taken(i).start()
    in_act.start()
    in_grads.start()
    for i in range(parts):
        taken(i).wait()
        broad[i] = narrow[i].astype(F32)
        given(i).start()
    in_act.wait()
    out_act.start()
    in_grads.wait()
    for copy in out_grads:
        copy.start()
    for i in range(parts):
        given(i).wait()
    out_act.wait()
    for copy in out_grads:
        copy.wait()


def per_device(
    tokens, cotangent, segment_ids, pad_mask, prefix_keys, prefix_values,
    w_query, w_key, w_value, w_out, w_up, w_down_t,
    norm1_gain, norm1_bias, norm2_gain, norm2_bias,
):
    rows, keys = lax.axis_size("rows"), lax.axis_size("keys")
    assert keys == KEYS and rows % (2 * KEYS) == 0 and rows & (rows - 1) == 0
    tok, width = tokens.shape[1:]
    count = prefix_keys.shape[1]
    prefix = count * keys
    local_ff = w_up.shape[2]
    wide, own, window = width // keys, tok // keys, 3 * tok // keys
    heads = wide // HEAD
    nz, bits, pieces = rows // 2, rows.bit_length() - 1, 4 * LAYERS
    vmem, anywhere = pl.BlockSpec(memory_space=pltpu.VMEM), pl.BlockSpec(memory_space=pl.ANY)
    dma = pltpu.SemaphoreType.DMA
    scratch = [
        pltpu.VMEM((LAYERS, width, 3 * wide), BF),
        pltpu.VMEM((LAYERS, wide, width), BF),
        pltpu.VMEM((LAYERS, width, local_ff), BF),
        pltpu.VMEM((LAYERS, width, local_ff), BF),
        pltpu.VMEM((LAYERS, prefix, wide), BF),
        pltpu.VMEM((LAYERS, prefix, wide), BF),
        pltpu.VMEM((tok, width), BF),
        pltpu.VMEM((SCATTERS, 2, own, width), BF),
        pltpu.VMEM((SCATTERS, own, width), BF),
        pltpu.VMEM((own, width), BF),
        pltpu.VMEM((GATHERS, tok, width), BF),
        pltpu.VMEM((LAYERS, tok, 3 * wide), BF),
        pltpu.VMEM((LAYERS, keys, prefix + window, heads * own), F32),
        pltpu.VMEM((LAYERS, tok, local_ff), F32),
        pltpu.VMEM((2 * LAYERS, own, width), F32),
        pltpu.VMEM((2 * LAYERS, own, 1), F32),
        pltpu.VMEM((own, width), F32),
        pltpu.VMEM((own, width), F32),
        pltpu.VMEM((own, width), F32),
        pltpu.VMEM((own, width), BF),
        pltpu.VMEM((tok, wide), BF),
        pltpu.VMEM((tok, 3 * wide), BF),
        pltpu.VMEM((prefix + tok, wide), F32),
        pltpu.VMEM((prefix + tok, wide), F32),
        pltpu.VMEM((tok, local_ff), BF),
        pltpu.VMEM((tok, wide), BF),
        pltpu.VMEM((keys, window, own), F32),
        pltpu.VMEM((tok, own), F32),
        pltpu.VMEM((LAYERS, 2, count, width), F32),
        pltpu.VMEM((LAYERS, 2, count, width), BF),
        pltpu.VMEM((LAYERS, bits, 2, count, width), BF),
        dma((pieces, 2, nz + 1)),
        dma((pieces, 2, nz)),
        dma((pieces, nz)),
        dma((16,)),
        dma((2, keys)),
        dma((2, keys)),
        dma((2 * SUBS + 1,)),
        dma((2 * SUBS + 1,)),
        dma((2, 2 * SUBS + 1)),
        dma((2, 2 * SUBS + 1)),
        dma((2, keys)),
        dma((2, keys)),
        dma((LAYERS, bits)),
        dma((LAYERS, bits)),
    ]
    low, grads = pl.pallas_call(
        functools.partial(kernel, (rows, tok, width, local_ff)),
        out_shape=(
            jax.ShapeDtypeStruct((2, tok, width), BF),
            jax.ShapeDtypeStruct((2, LAYERS, count, width), F32),
        ),
        in_specs=[vmem, anywhere, vmem, vmem] + [anywhere] * 8 + [vmem] * 4,
        out_specs=(anywhere, vmem),
        scratch_shapes=scratch,
        compiler_params=pltpu.CompilerParams(
            collective_id=0, has_side_effects=True, vmem_limit_bytes=62 * 1024 * 1024 - 512 * 1024
        ),
    )(
        tokens[0], cotangent[0], segment_ids, pad_mask, prefix_keys, prefix_values,
        w_query, w_key, w_value, w_out, w_up, w_down_t,
        norm1_gain, norm1_bias, norm2_gain, norm2_bias,
    )
    whole = (LAYERS, count, width)
    return pl.pallas_call(
        results,
        out_shape=(
            jax.ShapeDtypeStruct((1, tok, width), BF),
            jax.ShapeDtypeStruct((1, tok, width), F32),
            jax.ShapeDtypeStruct(whole, F32),
            jax.ShapeDtypeStruct(whole, F32),
        ),
        in_specs=[anywhere] * 2,
        out_specs=(anywhere,) * 4,
        scratch_shapes=[
            pltpu.VMEM((keys, own, width), BF),
            pltpu.VMEM((keys, own, width), F32),
            pltpu.VMEM((tok, width), BF),
            pltpu.VMEM((2, *whole), F32),
            dma((3, keys)),
        ],
    )(low, grads)


def solution(mesh):
    row3 = P("rows", None, None)
    weight = P(None, "rows", None)
    return jax.shard_map(
        per_device,
        mesh=mesh,
        in_specs=(
            row3,
            row3,
            P("rows", None),
            P("rows", None),
            P(None, "keys", None),
            P(None, "keys", None),
            weight,
            weight,
            weight,
            weight,
            P(None, "rows", "keys"),
            P(None, "rows", "keys"),
            P(),
            P(),
            P(),
            P(),
        ),
        out_specs=(row3, row3, P(None, "keys", None), P(None, "keys", None)),
        check_vma=False,
    )
```

time: 288 us -> 251 us (0.87)
  Pallas kernels: 280 us -> 250 us
  local copies, waits for them, and re-layouts: 5.91 us -> 0 us
    pallas_call x1, Pallas kernels: 280 us -> 247 us  [per_device(): pl.pallas_call(functools.partial(kernel, (rows, tok, width, local_ff)), o...]
    unnamed x10 -> x0, local copies, waits for them, and re-layouts: 5.05 us -> none
where the time goes in v3:
time: 251 us; the launch traced here: 250 us
  Pallas kernels  250 us (100%)
    pallas_call x1, Pallas kernels, per_device(): pl.pallas_call(functools.partial(kernel, (rows, tok, width, local_ff)), o...  247 us

profile of v3, /device:TPU:1, one launch (start us, length us, event | category | flops | bytes accessed | tf_op | source)
XLA Modules:
  0.0 250.4 jit_solution(2028219373548672152)
XLA Ops:
  0.6 246.7 %shard_map.183 = (bf16[2,512,1024]{2,1,0:T(8,128)(2,1)}, f32[2,2,16,1024]{3,2,1,0:T(8,128)}) custom-call(bf16[512,1024]{1,0:T(8,128)(2,1)} %bitcast.2, bf16[512,1024]{1,0:T(8,128)(2,1)} %bitcast.3, s32[1,512]{1,0:T(1,128)} %segments.1, s32[1,512]{1,0:T(1,128)} %padding.1, bf16[2,16,1024]{2,1,0:T(8,128)(2,1)} %pre_k.1, bf16[2,16,1024]{2,1,0:T(8,128)(2,1)} %pre_v.1, ...), custom_call_target="tpu_custom_call" | custom-call | tf_op jit(solution)/shard_map/pallas_call | solution.py:859
  247.4 2.8 %shard_map.184 = (bf16[1,512,1024]{2,1,0:T(8,128)(2,1)}, f32[1,512,1024]{2,1,0:T(8,128)}, f32[2,16,1024]{2,1,0:T(8,128)}, f32[2,16,1024]{2,1,0:T(8,128)}) custom-call(bf16[2,512,1024]{2,1,0:T(8,128)(2,1)} %get-tuple-element.6.low, f32[2,2,16,1024]{3,2,1,0:T(8,128)} %get-tuple-element.7.grads), custom_call_target="tpu_custom_call" | custom-call | tf_op jit(solution)/shard_map/pallas_call | solution.py:877

commit v4 on v3

--- a/solution.py
+++ b/solution.py
@@ -22,6 +22,115 @@
 SCATTERS = 8
 GATHER_BEFORE = (None, AG_M0, AG_X1, AG_M1, AG_GF1, AG_GA1, AG_GF0, AG_GA0)
 SUBS = 4
+
+SCHEDULE = {
+    (0, "start"): (
+        ("beside", 1, 0),
+        ("beside", 7, 0),
+        ("along", 1, 0),
+        ("beside", 2, 0),
+        ("along", 0, 0),
+        ("down", 1, 1),
+        ("along", 4, 0),
+        ("up", 1, 1),
+        ("down", 0, 1),
+        ("up", 0, 1),
+        ("up", 1, 2),
+        ("down", 1, 2),
+        ("along", 2, 0),
+        ("up", 0, 2),
+        ("up", 1, 3),
+        ("beside", 0, 0),
+        ("down", 0, 2),
+        ("up", 2, 1),
+        ("down", 1, 3),
+        ("down", 2, 1),
+        ("up", 0, 3),
+        ("along", 5, 0),
+        ("up", 2, 2),
+        ("down", 0, 3),
+        ("along", 3, 0),
+        ("down", 2, 2),
+        ("up", 2, 3),
+        ("down", 3, 1),
+        ("down", 5, 1),
+        ("up", 3, 1),
+        ("up", 3, 2),
+    ),
+    (0, "attended b"): (
+        ("up", 5, 2),
+    ),
+    (0, "out b"): (
+        ("beside", 5, 0),
+        ("up", 5, 1),
+        ("along", 6, 0),
+    ),
+    (0, "out a"): (
+        ("beside", 3, 0),
+        ("down", 3, 2),
+        ("down", 5, 2),
+        ("down", 2, 3),
+    ),
+    (0, "norm 3"): (
+        ("up", 4, 1),
+        ("up", 3, 3),
+        ("up", 4, 2),
+        ("down", 4, 1),
+    ),
+    (0, "normed"): (
+        ("up", 4, 3),
+        ("swap", 7, 0),
+    ),
+    (0, "up"): (
+        ("down", 3, 3),
+        ("down", 4, 2),
+    ),
+    (0, "up far"): (
+        ("along", 7, 0),
+    ),
+    (0, "down 0"): (
+        ("beside", 4, 0),
+    ),
+    (0, "down 1"): (
+        ("up", 6, 1),
+    ),
+    (0, "down 2"): (
+        ("down", 5, 3),
+        ("up", 5, 3),
+    ),
+    (0, "last norm 1"): (
+        ("down", 4, 3),
+        ("down", 6, 1),
+    ),
+    (0, "last norm 2"): (
+        ("up", 6, 2),
+        ("down", 6, 2),
+    ),
+    (1, "start"): (
+        ("beside", 6, 0),
+        ("down", 7, 1),
+    ),
+    (1, "projected near"): (
+        ("up", 7, 1),
+    ),
+    (1, "out b"): (
+        ("up", 6, 3),
+    ),
+    (1, "out a"): (
+        ("down", 6, 3),
+    ),
+    (1, "norm 1"): (
+        ("down", 7, 2),
+    ),
+    (1, "norm 2"): (
+        ("up", 7, 2),
+    ),
+    (1, "up far"): (
+        ("up", 7, 3),
+        ("down", 7, 3),
+    ),
+}
+STRAIGHT = (7,)
 
 
 def dot_nn(a, b):
@@ -135,7 +244,7 @@
         )
 
     def straight(p):
-        return p == 4 * LAYERS - 1
+        return p in STRAIGHT
 
     def up(p, zz, xx):
         return push(p, zz, xx, w_send.at[p, xx, zz], (lax.rem(z + 1, nz) * 2 + x, k))
@@ -277,8 +386,6 @@
     lax.fori_loop(0, own // 16, widen, 0)
     pl.semaphore_wait(barrier, nz - 1 + 1 + KEYS - 1)
     own_wait(0)
-    issue(0)
-    beside_own(0)
     for i in range(2):
         for d in range(1, KEYS):
             pre_copy(i, d).start()
@@ -326,11 +433,12 @@
         mine = part[rows_at(k * own + at, 16), :].astype(F32) + rc[n, 1, at : at + 16, :].astype(F32)
         return mine + ry[n, at : at + 16, :].astype(F32)
 
-    def rs_each(n, body, target):
+    def rs_each(n, body, target, between=lambda i: None):
         if n > 0:
             ag_end(GATHER_BEFORE[n])
         rs_copy(n, SUBS).wait_recv()
         for i in range(SUBS):
+            between(i)
             rs_copy(n, SUBS + 1 + i).wait_recv()
             for at in range(i * sub, (i + 1) * sub, 16):
                 body(at)
@@ -470,8 +578,9 @@
         gu = (dot_nn(gradient, wd[layer]) * slope).astype(BF)
         return dot_nt(gu, wu[layer]).astype(BF)
 
-    def scatter_far(n, step):
+    def scatter_far(n, step, between=lambda i: None):
         for i in range(SUBS):
+            between(i)
             value = step(i)
             at_a, at_b = far_rows(i)
             part[at_b, :] = value[sub:]
@@ -518,83 +627,88 @@
 
         return body
 
-    for i in range(2):
-        pre_own(i).wait()
-        for d in range(1, KEYS):
-            pre_copy(i, d).wait_recv()
-
-    def forward_layer(layer, first, second, third, fourth, fifth):
+    def weights_at(layer, point):
+        for kind, p, distance in SCHEDULE.get((layer, point), ()):
+            if kind == "along":
+                issue(p)
+            elif kind == "beside":
+                beside_own(p)
+            elif kind == "swap":
+                swap(p)
+            else:
+                passes(p, distance - 1, (kind == "up",))
+
+    def forward_layer(layer):
         base = 4 * layer
         rs_a, rs_f = ((RS_A0, RS_F0), (RS_A1, RS_F1))[layer]
         ag_m = (AG_M0, AG_M1)[layer]
         source = tokens if layer == 0 else full.at[AG_X1]
-        first()
+        here = functools.partial(weights_at, layer)
+        here("start")
         arrive(base)
         if layer > 0:
             ag_near(AG_X1)
         project(layer, source, near)
+        here("projected near")
+        if layer == 0:
+            for i in range(2):
+                pre_own(i).wait()
+                for d in range(1, KEYS):
+                    pre_copy(i, d).wait_recv()
         if layer > 0:
             ag_far(AG_X1)
         project(layer, source, far)
-        second()
+        here("projected")
         attend(layer, block_b)
+        here("attended b")
         arrive(base + 1)
         out_rows(layer, block_b * own, own)
         for i in range(SUBS):
             rs_copy(rs_a, i).start()
+        here("out b")
         attend(layer, block_a)
         out_rows(layer, block_a * own, own)
         for i in range(SUBS):
             rs_mid(rs_a, i)
+        here("out a")
         two(functools.partial(attend, layer), near)
         out_rows(layer, near * half, half)
         rs_near(rs_a)
-        third()
-        rs_each(rs_a, norm_into(rs_a, own_x, layer, 0, g1, b1, own_m, ag_m), ag_m)
-        fourth()
+        here("out near")
+        rs_each(
+            rs_a,
+            norm_into(rs_a, own_x, layer, 0, g1, b1, own_m, ag_m),
+            ag_m,
+            lambda i: here(f"norm {i}"),
+        )
+        here("normed")
         arrive(base + 2)
         ag_near(ag_m)
+        here("up")
         up_half(layer, ag_m, near)
+        here("up near")
         ag_far(ag_m)
         up_half(layer, ag_m, far)
-        fifth()
+        here("up far")
         arrive(base + 3)
-        scatter_far(rs_f, lambda i: dot_nt(both(hid, at=far_rows(i)), wd[layer]).astype(BF))
+        here("down")
+        scatter_far(
+            rs_f,
+            lambda i: dot_nt(both(hid, at=far_rows(i)), wd[layer]).astype(BF),
+            lambda i: here(f"down {i}"),
+        )
         part[half_rows(near), :] = dot_nt(hid[half_rows(near), :], wd[layer]).astype(BF)
         rs_near(rs_f)
-
-    def events(*calls):
-        def run():
-            for call in calls:
-                if len(call) == 1:
-                    issue(call[0])
-                    beside_own(call[0])
-                elif call[1] == 0:
-                    swap(call[0])
-                else:
-                    passes(call[0], call[1] - 1, (True, False))
-
-        return run
-
-    events((1,), (2,))()
-    forward_layer(
-        0,
-        events((0, 1), (0, 2), (0, 3), (1, 1), (3,)),
-        events((1, 2), (1, 3), (2, 1)),
-        events((2, 2), (2, 3), (3, 1), (4,)),
-        events((3, 2), (3, 3), (4, 1), (5,)),
-        events((4, 2), (4, 3), (5, 1), (6,)),
+        here("down near")
+
+    forward_layer(0)
+    rs_each(
+        RS_F0,
+        norm_into(RS_F0, own_m, 0, 1, g2, b2, own_x, AG_X1),
+        AG_X1,
+        lambda i: weights_at(0, f"last norm {i}"),
     )
-    events((5, 2), (5, 3), (6, 1), (7,))()
-    rs_each(RS_F0, norm_into(RS_F0, own_m, 0, 1, g2, b2, own_x, AG_X1), AG_X1)
-    forward_layer(
-        1,
-        events((6, 2), (7, 0), (6, 3)),
-        events(),
-        events((7, 1)),
-        events((7, 2)),
-        events((7, 3)),
-    )
+    forward_layer(1)
 
     def prefix_copy(layer, i, d):
         kt = lax.rem(k + d, KEYS)

time: 251 us -> 228 us (0.908)
  Pallas kernels: 250 us -> 227 us
    pallas_call x1, Pallas kernels: 247 us -> 224 us  [per_device(): pl.pallas_call(functools.partial(kernel, (rows, tok, width, local_ff)), o...]
where the time goes in v4:
time: 228 us
  Pallas kernels  227 us (100%)
    pallas_call x1, Pallas kernels, per_device(): pl.pallas_call(functools.partial(kernel, (rows, tok, width, local_ff)), o...  224 us

profile of v4, /device:TPU:1, one launch (start us, length us, event | category | flops | bytes accessed | tf_op | source)
XLA Modules:
  0.0 228.1 jit_solution(16182499029715182919)
XLA Ops:
  0.6 224.5 %shard_map.183 = (bf16[2,512,1024]{2,1,0:T(8,128)(2,1)}, f32[2,2,16,1024]{3,2,1,0:T(8,128)}) custom-call(bf16[512,1024]{1,0:T(8,128)(2,1)} %bitcast.2, bf16[512,1024]{1,0:T(8,128)(2,1)} %bitcast.3, s32[1,512]{1,0:T(1,128)} %segments.1, s32[1,512]{1,0:T(1,128)} %padding.1, bf16[2,16,1024]{2,1,0:T(8,128)(2,1)} %pre_k.1, bf16[2,16,1024]{2,1,0:T(8,128)(2,1)} %pre_v.1, ...), custom_call_target="tpu_custom_call" | custom-call | tf_op jit(solution)/shard_map/pallas_call | solution.py:973
  225.1 2.8 %shard_map.184 = (bf16[1,512,1024]{2,1,0:T(8,128)(2,1)}, f32[1,512,1024]{2,1,0:T(8,128)}, f32[2,16,1024]{2,1,0:T(8,128)}, f32[2,16,1024]{2,1,0:T(8,128)}) custom-call(bf16[2,512,1024]{2,1,0:T(8,128)(2,1)} %get-tuple-element.6.low, f32[2,2,16,1024]{3,2,1,0:T(8,128)} %get-tuple-element.7.grads), custom_call_target="tpu_custom_call" | custom-call | tf_op jit(solution)/shard_map/pallas_call | solution.py:991

commit v5 on v4

--- a/solution.py
+++ b/solution.py
@@ -16,12 +16,12 @@
 BF = jnp.bfloat16
 F32 = jnp.float32
 
-AG_M0, AG_X1, AG_M1, AG_GF1, AG_GA1, AG_GF0, AG_GA0, AG_GX, AG_ACT = range(9)
-GATHERS = 9
+AG_M0, AG_X1, AG_M1, AG_GF1, AG_GF0, AG_GX, AG_ACT = range(7)
+GATHERS = 7
 RS_A0, RS_F0, RS_A1, RS_F1, RS_GM1, RS_GX1, RS_GM0, RS_GX0 = range(8)
 SCATTERS = 8
-GATHER_BEFORE = (None, AG_M0, AG_X1, AG_M1, AG_GF1, AG_GA1, AG_GF0, AG_GA0)
-SUBS = 4
+GATHER_BEFORE = (None, AG_M0, AG_X1, AG_M1, AG_GF1, None, AG_GF0, None)
+SUBS = 2
 
 SCHEDULE = {
     (0, "start"): (
@@ -71,7 +71,7 @@
         ("down", 5, 2),
         ("down", 2, 3),
     ),
-    (0, "norm 3"): (
+    (0, "norm 1"): (
         ("up", 4, 1),
         ("up", 3, 3),
         ("up", 4, 2),
@@ -90,19 +90,17 @@
     ),
     (0, "down 0"): (
         ("beside", 4, 0),
+        ("up", 6, 1),
     ),
     (0, "down 1"): (
-        ("up", 6, 1),
-    ),
-    (0, "down 2"): (
         ("down", 5, 3),
         ("up", 5, 3),
     ),
-    (0, "last norm 1"): (
+    (0, "last norm 0"): (
         ("down", 4, 3),
         ("down", 6, 1),
     ),
-    (0, "last norm 2"): (
+    (0, "last norm 1"): (
         ("up", 6, 2),
         ("down", 6, 2),
     ),
@@ -119,10 +117,10 @@
     (1, "out a"): (
         ("down", 6, 3),
     ),
+    (1, "norm 0"): (
+        ("down", 7, 2),
+    ),
     (1, "norm 1"): (
-        ("down", 7, 2),
-    ),
-    (1, "norm 2"): (
         ("up", 7, 2),
     ),
     (1, "up far"): (
@@ -154,9 +152,10 @@
     wqkv, wo, wu, wd, pk, pv,
     part, rc, ry, ys, full,
     qkv, prob, gelu_d, zhat, rinv,
-    own_x, own_m, own_g, cot, att, gqkv, gk, gv, hid, go, bias, codes,
+    own_x, own_m, own_g, cot, att, gqkv, gk, gv, hid, ga, go_all, go, bias, codes,
     pg, pg_low, pg_in,
     w_send, w_recv, w_over, loc, pre_send, pre_recv,
+    wq_send, wq_recv, go_send, go_recv,
     rs_send, rs_recv, ag_send, ag_recv, pg_send, pg_recv, pgr_send, pgr_recv,
 ):
     rows, tok, width, local_ff = dims
@@ -194,7 +193,6 @@
         pl.semaphore_signal(barrier, inc=1, device_id=(r, lax.rem(k + d, KEYS)), device_id_type=MESH)
 
     group = nz // KEYS
-    first_row = k * (rows // KEYS)
 
     def spot(ref, layer, at):
         return ref.at[layer, pl.ds(pl.multiple_of(at * depth, depth), depth), :]
@@ -202,9 +200,7 @@
     def slot(p, zz, xx):
         layer, kind = divmod(p, 4)
         at = zz * 2 + xx
-        if kind == 1:
-            return spot(wo, layer, at - first_row)
-        return spot((wqkv, None, wu, wd)[kind], layer, at)
+        return spot((wqkv, wo, wu, wd)[kind], layer, at)
 
     def active(p, zz):
         return None if p % 4 != 1 else (zz // group) == k
@@ -433,8 +429,8 @@
         mine = part[rows_at(k * own + at, 16), :].astype(F32) + rc[n, 1, at : at + 16, :].astype(F32)
         return mine + ry[n, at : at + 16, :].astype(F32)
 
-    def rs_each(n, body, target, between=lambda i: None):
-        if n > 0:
+    def rs_each(n, body, leave, between=lambda i: None):
+        if GATHER_BEFORE[n] is not None:
             ag_end(GATHER_BEFORE[n])
         rs_copy(n, SUBS).wait_recv()
         for i in range(SUBS):
@@ -442,9 +438,16 @@
             rs_copy(n, SUBS + 1 + i).wait_recv()
             for at in range(i * sub, (i + 1) * sub, 16):
                 body(at)
-            ag_copy(target, i).start()
-        ag_copy(target, SUBS).start()
+            leave(i)
         rs_end(n)
+
+    def gather(n):
+        def leave(i):
+            ag_copy(n, i).start()
+            if i == SUBS - 1:
+                ag_copy(n, SUBS).start()
+
+        return leave
 
     def rs_end(n):
         for i in range(2 * SUBS + 1):
@@ -561,7 +564,7 @@
 
     def out_rows(layer, at, size):
         rows_here = rows_at(at, size)
-        part[rows_here, :] = dot_nn(att[rows_here, :], wo[layer]).astype(BF)
+        part[rows_here, :] = dot_nn(att[rows_here, :], wo[layer, columns, :]).astype(BF)
 
     def up_half(layer, n, which):
         hr = half_rows(which)
@@ -611,7 +614,13 @@
 
         return body
 
-    def norm_back(read, layer, which, gain, target):
+    def into(n):
+        def store(i, low):
+            full[n, rows_at(k * own + i, 16), :] = low
+
+        return store
+
+    def norm_back(read, layer, which, gain, store):
         index = 2 * layer + which
         g = gain[layer : layer + 1, :]
 
@@ -623,9 +632,53 @@
             second = jnp.mean(scaled * hat, axis=-1, keepdims=True)
             result = inv * (scaled - first - hat * second)
             own_g[i : i + 16, :] = result
-            full[target, rows_at(k * own + i, 16), :] = result.astype(BF)
+            store(i, result.astype(BF))
 
         return body
+
+    quarter = width // KEYS
+
+    def quarter_copy(layer, i):
+        at = (k, k, lax.rem(k + 2, KEYS))[i]
+        place = wo.at[layer, pl.ds(pl.multiple_of(at * quarter, quarter), quarter), :]
+        return pltpu.make_async_remote_copy(
+            src_ref=place, dst_ref=place, send_sem=wq_send.at[layer, i], recv_sem=wq_recv.at[layer, i],
+            device_id=(across, sib, sib)[i], device_id_type=MESH,
+        )
+
+    def quarter_start(layer):
+        quarter_copy(layer, 0).start()
+        quarter_copy(layer, 1).start()
+
+    def quarter_pass(layer):
+        quarter_copy(layer, 0).wait_recv()
+        quarter_copy(layer, 2).start()
+
+    def quarter_got(layer):
+        quarter_copy(layer, 1).wait_recv()
+        quarter_copy(layer, 2).wait_recv()
+
+    def go_copy(d, i):
+        kt = lax.rem(k + d, KEYS)
+        return pltpu.make_async_remote_copy(
+            src_ref=go_all.at[i * sub : (i + 1) * sub, pl.ds(pl.multiple_of(kt * wide, wide), wide)],
+            dst_ref=go.at[rows_at(k * own + i * sub, sub), :],
+            send_sem=go_send.at[d, i], recv_sem=go_recv.at[d, i], device_id=(r, kt), device_id_type=MESH,
+        )
+
+    def go_leave(layer):
+        def leave(i):
+            at = slice(i * sub, (i + 1) * sub)
+            go_all[at, :] = dot_nt(ga[at, :], wo[layer]).astype(BF)
+            for d in (2, *range(1, KEYS, 2)):
+                go_copy(d, i).start()
+            go[rows_at(k * own + i * sub, sub), :] = go_all[at, columns]
+
+        return leave
+
+    def go_wait(d):
+        for i in range(SUBS):
+            go_copy(d, i).wait_recv()
 
     def weights_at(layer, point):
         for kind, p, distance in SCHEDULE.get((layer, point), ()):
@@ -678,10 +731,11 @@
         rs_each(
             rs_a,
             norm_into(rs_a, own_x, layer, 0, g1, b1, own_m, ag_m),
-            ag_m,
+            gather(ag_m),
             lambda i: here(f"norm {i}"),
         )
         here("normed")
+        quarter_start(layer)
         arrive(base + 2)
         ag_near(ag_m)
         here("up")
@@ -699,13 +753,15 @@
         )
         part[half_rows(near), :] = dot_nt(hid[half_rows(near), :], wd[layer]).astype(BF)
         rs_near(rs_f)
+        if layer == 0:
+            quarter_pass(0)
         here("down near")
 
     forward_layer(0)
     rs_each(
         RS_F0,
         norm_into(RS_F0, own_m, 0, 1, g2, b2, own_x, AG_X1),
-        AG_X1,
+        gather(AG_X1),
         lambda i: weights_at(0, f"last norm {i}"),
     )
     forward_layer(1)
@@ -770,18 +826,22 @@
 
     for layer in reversed(range(LAYERS)):
         rs_gm, rs_gx = ((RS_GM0, RS_GX0), (RS_GM1, RS_GX1))[layer]
-        ag_gf, ag_ga = ((AG_GF0, AG_GA0), (AG_GF1, AG_GA1))[layer]
+        ag_gf = (AG_GF0, AG_GF1)[layer]
         if layer == LAYERS - 1:
             forth = norm_into(RS_F1, own_m, 1, 1, g2, b2, own_x, AG_ACT)
-            back = norm_back(lambda i: cot[i : i + 16, :].astype(F32), layer, 1, g2, ag_gf)
+            back = norm_back(lambda i: cot[i : i + 16, :].astype(F32), layer, 1, g2, into(ag_gf))
 
             def turn(i):
                 forth(i)
                 back(i)
 
-            rs_each(RS_F1, turn, ag_gf)
+            rs_each(RS_F1, turn, gather(ag_gf))
         else:
-            rs_each(RS_GX1, norm_back(lambda i: own_g[i : i + 16, :] + rs_sum(RS_GX1, i), layer, 1, g2, ag_gf), ag_gf)
+            rs_each(
+                RS_GX1,
+                norm_back(lambda i: own_g[i : i + 16, :] + rs_sum(RS_GX1, i), layer, 1, g2, into(ag_gf)),
+                gather(ag_gf),
+            )
             prefix_take(layer + 1)
         ag_near(ag_gf)
         part[half_rows(near), :] = ff_back(layer, full[ag_gf, half_rows(near), :], gelu_d[layer, half_rows(near), :])
@@ -793,23 +853,36 @@
             at = far_rows(i)
             return ff_back(layer, both(full, ag_gf, at=at), both(gelu_d, layer, at=at))
 
+        if layer == LAYERS - 1:
+            quarter_pass(layer)
         scatter_far(rs_gm, step)
         if layer == 0:
             row_step(1, 0)
         gk[...] = jnp.zeros_like(gk)
         gv[...] = jnp.zeros_like(gv)
-        rs_each(rs_gm, norm_back(lambda i: own_g[i : i + 16, :] + rs_sum(rs_gm, i), layer, 0, g1, ag_ga), ag_ga)
+        quarter_got(layer)
+
+        def keep(i, low):
+            ga[i : i + 16, :] = low
+
+        rs_each(
+            rs_gm,
+            norm_back(lambda i: own_g[i : i + 16, :] + rs_sum(rs_gm, i), layer, 0, g1, keep),
+            go_leave(layer),
+        )
         if layer == LAYERS - 1:
             for i in range(SUBS + 1):
                 ag_copy(AG_ACT, i).start()
-        ag_near(ag_ga)
-        go[half_rows(near), :] = dot_nt(full[ag_ga, half_rows(near), :], wo[layer]).astype(BF)
+        go_wait(3 - 2 * c)
         two(functools.partial(attend_back, layer), near)
         if layer == 0:
             row_step(1, 1)
-        ag_far(ag_ga)
-        go[half_rows(far), :] = dot_nt(full[ag_ga, half_rows(far), :], wo[layer]).astype(BF)
+        go_wait(2)
+        go_wait(1 + 2 * c)
         two(functools.partial(attend_back, layer), far)
+        for d in range(1, KEYS):
+            for i in range(SUBS):
+                go_copy(d, i).wait_send()
         prefix_start(layer)
 
         def narrow(which):
@@ -845,7 +918,7 @@
     def last(i):
         full[AG_GX, rows_at(k * own + i, 16), :] = (own_g[i : i + 16, :] + rs_sum(RS_GX0, i)).astype(BF)
 
-    rs_each(RS_GX0, last, AG_GX)
+    rs_each(RS_GX0, last, gather(AG_GX))
     for p in range(4 * LAYERS):
         drain(p)
     for i in range(2):
@@ -869,6 +942,9 @@
             prefix_out[i, layer] = pg[layer, i]
     ag_end(AG_GX)
     ag_end(AG_ACT)
+    for layer in range(LAYERS):
+        for i in range(3):
+            quarter_copy(layer, i).wait_send()
     act_copy.wait()
     grad_copy(near).wait()
     grad_copy(far).wait()
@@ -925,7 +1001,7 @@
     dma = pltpu.SemaphoreType.DMA
     scratch = [
         pltpu.VMEM((LAYERS, width, 3 * wide), BF),
-        pltpu.VMEM((LAYERS, wide, width), BF),
+        pltpu.VMEM((LAYERS, width, width), BF),
         pltpu.VMEM((LAYERS, width, local_ff), BF),
         pltpu.VMEM((LAYERS, width, local_ff), BF),
         pltpu.VMEM((LAYERS, prefix, wide), BF),
@@ -949,6 +1025,8 @@
         pltpu.VMEM((prefix + tok, wide), F32),
         pltpu.VMEM((prefix + tok, wide), F32),
         pltpu.VMEM((tok, local_ff), BF),
+        pltpu.VMEM((own, width), BF),
+        pltpu.VMEM((own, width), BF),
         pltpu.VMEM((tok, wide), BF),
         pltpu.VMEM((keys, window, own), F32),
         pltpu.VMEM((tok, own), F32),
@@ -961,6 +1039,10 @@
         dma((16,)),
         dma((2, keys)),
         dma((2, keys)),
+        dma((LAYERS, 3)),
+        dma((LAYERS, 3)),
+        dma((keys, SUBS)),
+        dma((keys, SUBS)),
         dma((2 * SUBS + 1,)),
         dma((2 * SUBS + 1,)),
         dma((2, 2 * SUBS + 1)),

time: 228 us -> 223 us (0.978)
  Pallas kernels: 227 us -> 222 us
    pallas_call x1, Pallas kernels: 224 us -> 219 us  [per_device(): pl.pallas_call(functools.partial(kernel, (rows, tok, width, local_ff)), o...]
where the time goes in v5:
time: 223 us
  Pallas kernels  222 us (100%)
    pallas_call x1, Pallas kernels, per_device(): pl.pallas_call(functools.partial(kernel, (rows, tok, width, local_ff)), o...  219 us

profile of v5, /device:TPU:1, one launch (start us, length us, event | category | flops | bytes accessed | tf_op | source)
XLA Modules:
  0.0 223.1 jit_solution(6902537429220441470)
XLA Ops:
  0.6 219.4 %shard_map.183 = (bf16[2,512,1024]{2,1,0:T(8,128)(2,1)}, f32[2,2,16,1024]{3,2,1,0:T(8,128)}) custom-call(bf16[512,1024]{1,0:T(8,128)(2,1)} %bitcast.2, bf16[512,1024]{1,0:T(8,128)(2,1)} %bitcast.3, s32[1,512]{1,0:T(1,128)} %segments.1, s32[1,512]{1,0:T(1,128)} %padding.1, bf16[2,16,1024]{2,1,0:T(8,128)(2,1)} %pre_k.1, bf16[2,16,1024]{2,1,0:T(8,128)(2,1)} %pre_v.1, ...), custom_call_target="tpu_custom_call" | custom-call | tf_op jit(solution)/shard_map/pallas_call | solution.py:1055
  220.1 2.8 %shard_map.184 = (bf16[1,512,1024]{2,1,0:T(8,128)(2,1)}, f32[1,512,1024]{2,1,0:T(8,128)}, f32[2,16,1024]{2,1,0:T(8,128)}, f32[2,16,1024]{2,1,0:T(8,128)}) custom-call(bf16[2,512,1024]{2,1,0:T(8,128)(2,1)} %get-tuple-element.6.low, f32[2,2,16,1024]{3,2,1,0:T(8,128)} %get-tuple-element.7.grads), custom_call_target="tpu_custom_call" | custom-call | tf_op jit(solution)/shard_map/pallas_call | solution.py:1073

commit v6 on v5

--- a/solution.py
+++ b/solution.py
@@ -145,14 +145,14 @@
 
 def kernel(
     dims,
-    tokens, cotangent, segments, padding, pre_k, pre_v,
+    token_rows, cotangent, segments, padding, pre_k, pre_v,
     w_query, w_key, w_value, w_out, w_up, w_down,
     g1, b1, g2, b2,
     low_out, prefix_out,
     wqkv, wo, wu, wd, pk, pv,
     part, rc, ry, ys, full,
     qkv, prob, gelu_d, zhat, rinv,
-    own_x, own_m, own_g, cot, att, gqkv, gk, gv, hid, ga, go_all, go, bias, codes,
+    own_x, own_m, own_g, cot, att, gqkv, gk, gv, tokens, hid, ga, go_all, go, bias, codes,
     pg, pg_low, pg_in,
     w_send, w_recv, w_over, loc, pre_send, pre_recv,
     wq_send, wq_recv, go_send, go_recv,
@@ -360,6 +360,8 @@
     for p in range(4 * LAYERS):
         own_start(p)
     cot_copy.start()
+    token_copy = pltpu.make_async_copy(token_rows, tokens, loc.at[13])
+    token_copy.start()
     for i in range(2):
         pre_own(i).start()
 
@@ -369,7 +371,8 @@
     def mask_of(i, carry):
         queries = segments[:, pl.ds(pl.multiple_of(i * own, own), own)].astype(F32)
         keys_code = codes[pl.ds(pl.multiple_of(jnp.clip(i - 1, 0, KEYS - 3) * own, own), window), :]
-        bias[i] = jnp.where(keys_code == queries, 0.0, NEGATIVE)
+        bias[i, 0:prefix, :] = jnp.zeros((prefix, own), F32)
+        bias[i, prefix : prefix + window, :] = jnp.where(keys_code == queries, 0.0, NEGATIVE)
         return carry
 
     lax.fori_loop(0, KEYS, mask_of, 0)
@@ -379,6 +382,7 @@
         own_x[pl.ds(at, 16), :] = tokens[pl.ds(k * own + at, 16), :].astype(F32)
         return carry
 
+    token_copy.wait()
     lax.fori_loop(0, own // 16, widen, 0)
     pl.semaphore_wait(barrier, nz - 1 + 1 + KEYS - 1)
     own_wait(0)
@@ -518,42 +522,39 @@
         parts = [value[h * HEAD : (h + 1) * HEAD, h * own : (h + 1) * own] for h in range(heads)]
         return jnp.concatenate(parts, axis=0).T
 
+    def seen(layer, start):
+        span = pl.ds(start, window)
+        return (
+            jnp.concatenate([pk[layer], qkv[layer, span, wide : 2 * wide]], axis=0),
+            jnp.concatenate([pv[layer], qkv[layer, span, 2 * wide : 3 * wide]], axis=0),
+        )
+
     def attend(layer, i):
         q4 = stacked(qkv[layer, pl.ds(place_of(i), own), 0:wide])
-        span = pl.ds(window_of(i), window)
-        mask = bias[i]
-        s_tok = dot_nt(qkv[layer, span, wide : 2 * wide], q4) + jnp.concatenate([mask] * heads, axis=1)
-        s_pre = dot_nt(pk[layer], q4)
-        top = jnp.maximum(jnp.max(s_tok, axis=0, keepdims=True), jnp.max(s_pre, axis=0, keepdims=True))
-        e_tok, e_pre = jnp.exp(s_tok - top), jnp.exp(s_pre - top)
-        inverse = 1.0 / (jnp.sum(e_tok, axis=0, keepdims=True) + jnp.sum(e_pre, axis=0, keepdims=True))
-        p_tok, p_pre = e_tok * inverse, e_pre * inverse
-        prob[layer, i, 0:prefix, :] = p_pre
-        prob[layer, i, prefix : prefix + window, :] = p_tok
-        out = dot_tn(qkv[layer, span, 2 * wide : 3 * wide], p_tok.astype(BF))
-        out += dot_tn(pv[layer], p_pre.astype(BF))
-        att[pl.ds(place_of(i), own), :] = unstacked(out).astype(BF)
+        key_rows, value_rows = seen(layer, window_of(i))
+        s = dot_nt(key_rows, q4) + jnp.concatenate([bias[i]] * heads, axis=1)
+        e = jnp.exp(s - jnp.max(s, axis=0, keepdims=True))
+        p = e * (1.0 / jnp.sum(e, axis=0, keepdims=True))
+        prob[layer, i] = p
+        att[pl.ds(place_of(i), own), :] = unstacked(dot_tn(value_rows, p.astype(BF))).astype(BF)
 
     def attend_back(layer, i):
         at = pl.ds(place_of(i), own)
         q4 = stacked(qkv[layer, at, 0:wide])
         go4 = stacked(go[at, :])
         start = window_of(i)
-        span = pl.ds(start, window)
-        p_pre = prob[layer, i, 0:prefix, :]
-        p_tok = prob[layer, i, prefix : prefix + window, :]
-        gp_tok = dot_nt(qkv[layer, span, 2 * wide : 3 * wide], go4)
-        gp_pre = dot_nt(pv[layer], go4)
-        dsum = jnp.sum(p_tok * gp_tok, axis=0, keepdims=True) + jnp.sum(p_pre * gp_pre, axis=0, keepdims=True)
-        gs_tok = (p_tok * (gp_tok - dsum)).astype(BF)
-        gs_pre = (p_pre * (gp_pre - dsum)).astype(BF)
+        key_rows, value_rows = seen(layer, start)
+        p = prob[layer, i]
+        gp = dot_nt(value_rows, go4)
+        dsum = jnp.sum(p * gp, axis=0, keepdims=True)
+        gs = (p * (gp - dsum)).astype(BF)
         places = pl.ds(prefix + start, window)
-        gk[places, :] += dot_nn(gs_tok, q4)
-        gk[0:prefix, :] += dot_nn(gs_pre, q4)
-        gv[places, :] += dot_nn(p_tok.astype(BF), go4)
-        gv[0:prefix, :] += dot_nn(p_pre.astype(BF), go4)
-        gq = dot_tn(qkv[layer, span, wide : 2 * wide], gs_tok) + dot_tn(pk[layer], gs_pre)
-        gqkv[at, 0:wide] = (unstacked(gq).astype(BF).astype(F32) * HEAD**-0.5).astype(BF)
+        gk_here, gv_here = dot_nn(gs, q4), dot_nn(p.astype(BF), go4)
+        gk[0:prefix, :] += gk_here[:prefix]
+        gk[places, :] += gk_here[prefix:]
+        gv[0:prefix, :] += gv_here[:prefix]
+        gv[places, :] += gv_here[prefix:]
+        gqkv[at, 0:wide] = (unstacked(dot_tn(key_rows, gs)).astype(BF).astype(F32) * HEAD**-0.5).astype(BF)
 
     def two(body, which):
         def one(i, carry):
@@ -581,15 +582,17 @@
         gu = (dot_nn(gradient, wd[layer]) * slope).astype(BF)
         return dot_nt(gu, wu[layer]).astype(BF)
 
-    def scatter_far(n, step, between=lambda i: None):
+    def scatter_far(n, step, before=lambda i: None, early=False):
         for i in range(SUBS):
-            between(i)
+            before(i)
+            if early and i > 0:
+                rs_mid(n, i - 1)
             value = step(i)
             at_a, at_b = far_rows(i)
             part[at_b, :] = value[sub:]
             rs_copy(n, i).start()
             part[at_a, :] = value[:sub]
-            if i > 0:
+            if not early and i > 0:
                 rs_mid(n, i - 1)
         rs_mid(n, SUBS - 1)
 
@@ -848,14 +851,13 @@
         rs_near(rs_gm)
 
         def step(i):
-            ag_pass(ag_gf, i)
             ag_got(ag_gf, i)
             at = far_rows(i)
             return ff_back(layer, both(full, ag_gf, at=at), both(gelu_d, layer, at=at))
 
         if layer == LAYERS - 1:
             quarter_pass(layer)
-        scatter_far(rs_gm, step)
+        scatter_far(rs_gm, step, lambda i: ag_pass(ag_gf, i), early=True)
         if layer == 0:
             row_step(1, 0)
         gk[...] = jnp.zeros_like(gk)
@@ -918,13 +920,12 @@
     def last(i):
         full[AG_GX, rows_at(k * own + i, 16), :] = (own_g[i : i + 16, :] + rs_sum(RS_GX0, i)).astype(BF)
 
-    rs_each(RS_GX0, last, gather(AG_GX))
+    rs_each(RS_GX0, last, gather(AG_GX), lambda i: row_step(0, 0) if i == SUBS - 1 else None)
     for p in range(4 * LAYERS):
         drain(p)
     for i in range(2):
         for d in range(1, KEYS):
             pre_copy(i, d).wait_send()
-    row_step(0, 0)
     ag_near(AG_GX)
 
     def grad_copy(which):
@@ -1024,11 +1025,12 @@
         pltpu.VMEM((tok, 3 * wide), BF),
         pltpu.VMEM((prefix + tok, wide), F32),
         pltpu.VMEM((prefix + tok, wide), F32),
+        pltpu.VMEM((tok, width), BF),
         pltpu.VMEM((tok, local_ff), BF),
         pltpu.VMEM((own, width), BF),
         pltpu.VMEM((own, width), BF),
         pltpu.VMEM((tok, wide), BF),
-        pltpu.VMEM((keys, window, own), F32),
+        pltpu.VMEM((keys, prefix + window, own), F32),
         pltpu.VMEM((tok, own), F32),
         pltpu.VMEM((LAYERS, 2, count, width), F32),
         pltpu.VMEM((LAYERS, 2, count, width), BF),
@@ -1058,7 +1060,7 @@
             jax.ShapeDtypeStruct((2, tok, width), BF),
             jax.ShapeDtypeStruct((2, LAYERS, count, width), F32),
         ),
-        in_specs=[vmem, anywhere, vmem, vmem] + [anywhere] * 8 + [vmem] * 4,
+        in_specs=[anywhere, anywhere, vmem, vmem] + [anywhere] * 8 + [vmem] * 4,
         out_specs=(anywhere, vmem),
         scratch_shapes=scratch,
         compiler_params=pltpu.CompilerParams(

time: 223 us -> 220 us (0.987)
  Pallas kernels: 222 us -> 219 us
    pallas_call x1, Pallas kernels: 219 us -> 216 us  [per_device(): pl.pallas_call(functools.partial(kernel, (rows, tok, width, local_ff)), o...]
where the time goes in v6:
time: 220 us
  Pallas kernels  219 us (100%)
    pallas_call x1, Pallas kernels, per_device(): pl.pallas_call(functools.partial(kernel, (rows, tok, width, local_ff)), o...  216 us

profile of v6, /device:TPU:1, one launch (start us, length us, event | category | flops | bytes accessed | tf_op | source)
XLA Modules:
  0.0 219.6 jit_solution(6553920402470528399)
XLA Ops:
  0.6 215.9 %shard_map.183 = (bf16[2,512,1024]{2,1,0:T(8,128)(2,1)}, f32[2,2,16,1024]{3,2,1,0:T(8,128)}) custom-call(bf16[512,1024]{1,0:T(8,128)(2,1)} %bitcast.2, bf16[512,1024]{1,0:T(8,128)(2,1)} %bitcast.3, s32[1,512]{1,0:T(1,128)} %segments.1, s32[1,512]{1,0:T(1,128)} %padding.1, bf16[2,16,1024]{2,1,0:T(8,128)(2,1)} %pre_k.1, bf16[2,16,1024]{2,1,0:T(8,128)(2,1)} %pre_v.1, ...), custom_call_target="tpu_custom_call" | custom-call | tf_op jit(solution)/shard_map/pallas_call | solution.py:1057
  216.6 2.8 %shard_map.184 = (bf16[1,512,1024]{2,1,0:T(8,128)(2,1)}, f32[1,512,1024]{2,1,0:T(8,128)}, f32[2,16,1024]{2,1,0:T(8,128)}, f32[2,16,1024]{2,1,0:T(8,128)}) custom-call(bf16[2,512,1024]{2,1,0:T(8,128)(2,1)} %get-tuple-element.6.low, f32[2,2,16,1024]{3,2,1,0:T(8,128)} %get-tuple-element.7.grads), custom_call_target="tpu_custom_call" | custom-call | tf_op jit(solution)/shard_map/pallas_call | solution.py:1075

commit v7 on v6

--- a/solution.py
+++ b/solution.py
@@ -178,16 +178,17 @@
     beside = (r + 1 - 2 * x, k)
     far, near = 1 - y, y
 
-    def level(d):
-        return lax.rem(z + d, nz)
-
     barrier = pltpu.get_barrier_semaphore()
 
-    def greet(d, carry):
-        pl.semaphore_signal(barrier, inc=1, device_id=(level(d) * 2 + x, k), device_id_type=MESH)
-        return carry
-
-    lax.fori_loop(1, nz, greet, 0)
+    def greet(zz):
+        pl.semaphore_signal(barrier, inc=1, device_id=(zz * 2 + x, k), device_id_type=MESH)
+
+    not_top, not_bottom = z < nz - 1, z > 0
+    pl.when(not_top)(lambda: greet(lax.rem(z + 1, nz)))
+    pl.when(not_bottom)(lambda: greet(lax.rem(z + nz - 1, nz)))
+    far_partners = [1 << b for b in range(1, nz.bit_length() - 1)]
+    for bit in far_partners:
+        greet(z + bit - 2 * bit * lax.rem(z // bit, 2))
     pl.semaphore_signal(barrier, inc=1, device_id=beside, device_id_type=MESH)
     for d in range(1, KEYS):
         pl.semaphore_signal(barrier, inc=1, device_id=(r, lax.rem(k + d, KEYS)), device_id_type=MESH)
@@ -252,8 +253,6 @@
     def over(p, zz):
         return push(p, zz, x, w_over.at[p, zz], beside)
 
-    not_top, not_bottom = z < nz - 1, z > 0
-
     def spread_own(p, xx, action):
         pl.when(not_top)(lambda: action(up(p, z, xx)))
         pl.when(not_bottom)(lambda: action(down(p, z, xx)))
@@ -384,7 +383,8 @@
 
     token_copy.wait()
     lax.fori_loop(0, own // 16, widen, 0)
-    pl.semaphore_wait(barrier, nz - 1 + 1 + KEYS - 1)
+    ends = jnp.where(z == 0, 1, 0) + jnp.where(z == nz - 1, 1, 0)
+    pl.semaphore_wait(barrier, 2 - ends + len(far_partners) + 1 + KEYS - 1)
     own_wait(0)
     for i in range(2):
         for d in range(1, KEYS):
@@ -483,9 +483,11 @@
     def ag_got(n, i):
         ag_copy(n, SUBS + 1 + i).wait_recv()
 
-    def ag_far(n):
+    def ag_far(n, between=lambda: None):
         for i in range(SUBS):
             ag_pass(n, i)
+            if i == 0:
+                between()
         for i in range(SUBS):
             ag_got(n, i)
 
@@ -934,9 +936,9 @@
         )
 
     grad_copy(near).start()
-    ag_far(AG_GX)
+    ag_far(AG_GX, lambda: row_step(0, 1))
     grad_copy(far).start()
-    for b in range(1, bits):
+    for b in range(2, bits):
         row_step(0, b)
     for i in range(2):
         for layer in range(LAYERS):
@@ -1083,11 +1085,11 @@
         in_specs=[anywhere] * 2,
         out_specs=(anywhere,) * 4,
         scratch_shapes=[
-            pltpu.VMEM((keys, own, width), BF),
-            pltpu.VMEM((keys, own, width), F32),
+            pltpu.VMEM((2 * keys, own // 2, width), BF),
+            pltpu.VMEM((2 * keys, own // 2, width), F32),
             pltpu.VMEM((tok, width), BF),
             pltpu.VMEM((2, *whole), F32),
-            dma((3, keys)),
+            dma((3, 2 * keys)),
         ],
     )(low, grads)
 

time: 220 us -> 218 us (level)
  Pallas kernels: 219 us -> 216 us
    pallas_call x1, Pallas kernels: 216 us -> 213 us  [per_device(): pl.pallas_call(functools.partial(kernel, (rows, tok, width, local_ff)), o...]
where the time goes in v7:
time: 218 us; the launch traced here: 217 us
  Pallas kernels  216 us (99%)
    pallas_call x1, Pallas kernels, per_device(): pl.pallas_call(functools.partial(kernel, (rows, tok, width, local_ff)), o...  213 us

profile of v7, /device:TPU:1, one launch (start us, length us, event | category | flops | bytes accessed | tf_op | source)
XLA Modules:
  0.0 217.1 jit_solution(5045919879164453903)
XLA Ops:
  0.6 213.4 %shard_map.183 = (bf16[2,512,1024]{2,1,0:T(8,128)(2,1)}, f32[2,2,16,1024]{3,2,1,0:T(8,128)}) custom-call(bf16[512,1024]{1,0:T(8,128)(2,1)} %bitcast.2, bf16[512,1024]{1,0:T(8,128)(2,1)} %bitcast.3, s32[1,512]{1,0:T(1,128)} %segments.1, s32[1,512]{1,0:T(1,128)} %padding.1, bf16[2,16,1024]{2,1,0:T(8,128)(2,1)} %pre_k.1, bf16[2,16,1024]{2,1,0:T(8,128)(2,1)} %pre_v.1, ...), custom_call_target="tpu_custom_call" | custom-call | tf_op jit(solution)/shard_map/pallas_call | solution.py:1059
  214.0 2.9 %shard_map.184 = (bf16[1,512,1024]{2,1,0:T(8,128)(2,1)}, f32[1,512,1024]{2,1,0:T(8,128)}, f32[2,16,1024]{2,1,0:T(8,128)}, f32[2,16,1024]{2,1,0:T(8,128)}) custom-call(bf16[2,512,1024]{2,1,0:T(8,128)(2,1)} %get-tuple-element.6.low, f32[2,2,16,1024]{3,2,1,0:T(8,128)} %get-tuple-element.7.grads), custom_call_target="tpu_custom_call" | custom-call | tf_op jit(solution)/shard_map/pallas_call | solution.py:1077

commit v8 on v7

--- a/solution.py
+++ b/solution.py
@@ -644,24 +644,21 @@
     quarter = width // KEYS
 
     def quarter_copy(layer, i):
-        at = (k, k, lax.rem(k + 2, KEYS))[i]
-        place = wo.at[layer, pl.ds(pl.multiple_of(at * quarter, quarter), quarter), :]
+        at = (k, k, k, lax.rem(k + 2, KEYS))[i] * quarter + (quarter // 2 if i == 1 else 0)
+        place = wo.at[layer, rows_at(at, quarter // 2 if i < 2 else quarter), :]
         return pltpu.make_async_remote_copy(
             src_ref=place, dst_ref=place, send_sem=wq_send.at[layer, i], recv_sem=wq_recv.at[layer, i],
-            device_id=(across, sib, sib)[i], device_id_type=MESH,
-        )
-
-    def quarter_start(layer):
-        quarter_copy(layer, 0).start()
-        quarter_copy(layer, 1).start()
+            device_id=(across, across, sib, sib)[i], device_id_type=MESH,
+        )
 
     def quarter_pass(layer):
         quarter_copy(layer, 0).wait_recv()
-        quarter_copy(layer, 2).start()
+        quarter_copy(layer, 1).wait_recv()
+        quarter_copy(layer, 3).start()
 
     def quarter_got(layer):
-        quarter_copy(layer, 1).wait_recv()
         quarter_copy(layer, 2).wait_recv()
+        quarter_copy(layer, 3).wait_recv()
 
     def go_copy(d, i):
         kt = lax.rem(k + d, KEYS)
@@ -705,6 +702,8 @@
         here("start")
         arrive(base)
         if layer > 0:
+            arrive(base + 1)
+            quarter_copy(layer, 0).start()
             ag_near(AG_X1)
         project(layer, source, near)
         here("projected near")
@@ -719,7 +718,8 @@
         here("projected")
         attend(layer, block_b)
         here("attended b")
-        arrive(base + 1)
+        if layer == 0:
+            arrive(base + 1)
         out_rows(layer, block_b * own, own)
         for i in range(SUBS):
             rs_copy(rs_a, i).start()
@@ -740,7 +740,10 @@
             lambda i: here(f"norm {i}"),
         )
         here("normed")
-        quarter_start(layer)
+        if layer == 0:
+            quarter_copy(layer, 0).start()
+        quarter_copy(layer, 1).start()
+        quarter_copy(layer, 2).start()
         arrive(base + 2)
         ag_near(ag_m)
         here("up")
@@ -946,7 +949,7 @@
     ag_end(AG_GX)
     ag_end(AG_ACT)
     for layer in range(LAYERS):
-        for i in range(3):
+        for i in range(4):
             quarter_copy(layer, i).wait_send()
     act_copy.wait()
     grad_copy(near).wait()
@@ -1043,8 +1046,8 @@
         dma((16,)),
         dma((2, keys)),
         dma((2, keys)),
-        dma((LAYERS, 3)),
-        dma((LAYERS, 3)),
+        dma((LAYERS, 4)),
+        dma((LAYERS, 4)),
         dma((keys, SUBS)),
         dma((keys, SUBS)),
         dma((2 * SUBS + 1,)),

time: 218 us -> 216 us (level)
    pallas_call x1, Pallas kernels: 213 us -> 211 us  [per_device(): pl.pallas_call(functools.partial(kernel, (rows, tok, width, local_ff)), o...]
where the time goes in v8:
time: 216 us; the launch traced here: 214 us
  Pallas kernels  214 us (99%)
    pallas_call x1, Pallas kernels, per_device(): pl.pallas_call(functools.partial(kernel, (rows, tok, width, local_ff)), o...  211 us

profile of v8, /device:TPU:1, one launch (start us, length us, event | category | flops | bytes accessed | tf_op | source)
XLA Modules:
  0.0 214.4 jit_solution(14319753748302695594)
XLA Ops:
  0.6 210.7 %shard_map.183 = (bf16[2,512,1024]{2,1,0:T(8,128)(2,1)}, f32[2,2,16,1024]{3,2,1,0:T(8,128)}) custom-call(bf16[512,1024]{1,0:T(8,128)(2,1)} %bitcast.2, bf16[512,1024]{1,0:T(8,128)(2,1)} %bitcast.3, s32[1,512]{1,0:T(1,128)} %segments.1, s32[1,512]{1,0:T(1,128)} %padding.1, bf16[2,16,1024]{2,1,0:T(8,128)(2,1)} %pre_k.1, bf16[2,16,1024]{2,1,0:T(8,128)(2,1)} %pre_v.1, ...), custom_call_target="tpu_custom_call" | custom-call | tf_op jit(solution)/shard_map/pallas_call | solution.py:1062
  211.4 2.9 %shard_map.184 = (bf16[1,512,1024]{2,1,0:T(8,128)(2,1)}, f32[1,512,1024]{2,1,0:T(8,128)}, f32[2,16,1024]{2,1,0:T(8,128)}, f32[2,16,1024]{2,1,0:T(8,128)}) custom-call(bf16[2,512,1024]{2,1,0:T(8,128)(2,1)} %get-tuple-element.6.low, f32[2,2,16,1024]{3,2,1,0:T(8,128)} %get-tuple-element.7.grads), custom_call_target="tpu_custom_call" | custom-call | tf_op jit(solution)/shard_map/pallas_call | solution.py:1080

commit v9 on v8

--- a/solution.py
+++ b/solution.py
@@ -244,10 +244,10 @@
         return p in STRAIGHT
 
     def up(p, zz, xx):
-        return push(p, zz, xx, w_send.at[p, xx, zz], (lax.rem(z + 1, nz) * 2 + x, k))
+        return push(p, zz, xx, w_send.at[p if xx is x else 4 * LAYERS, zz], (lax.rem(z + 1, nz) * 2 + x, k))
 
     def down(p, zz, xx):
-        sem = w_send.at[p, xx, jnp.where(zz == z, nz, zz)]
+        sem = w_send.at[p if xx is x else 4 * LAYERS, jnp.where(zz == z, nz, zz)]
         return push(p, zz, xx, sem, (lax.rem(z + nz - 1, nz) * 2 + x, k))
 
     def over(p, zz):
@@ -1040,7 +1040,7 @@
         pltpu.VMEM((LAYERS, 2, count, width), F32),
         pltpu.VMEM((LAYERS, 2, count, width), BF),
         pltpu.VMEM((LAYERS, bits, 2, count, width), BF),
-        dma((pieces, 2, nz + 1)),
+        dma((pieces + 1, nz + 1)),
         dma((pieces, 2, nz)),
         dma((pieces, nz)),
         dma((16,)),

time: 216 us -> 215 us (level)
  no operation moved by 1% of the time
where the time goes in v9:
time: 215 us; the launch traced here: 214 us
  Pallas kernels  213 us (99%)
    pallas_call x1, Pallas kernels, per_device(): pl.pallas_call(functools.partial(kernel, (rows, tok, width, local_ff)), o...  210 us

profile of v9, /device:TPU:1, one launch (start us, length us, event | category | flops | bytes accessed | tf_op | source)
XLA Modules:
  0.0 214.1 jit_solution(10480448484756794617)
XLA Ops:
  0.6 210.4 %shard_map.183 = (bf16[2,512,1024]{2,1,0:T(8,128)(2,1)}, f32[2,2,16,1024]{3,2,1,0:T(8,128)}) custom-call(bf16[512,1024]{1,0:T(8,128)(2,1)} %bitcast.2, bf16[512,1024]{1,0:T(8,128)(2,1)} %bitcast.3, s32[1,512]{1,0:T(1,128)} %segments.1, s32[1,512]{1,0:T(1,128)} %padding.1, bf16[2,16,1024]{2,1,0:T(8,128)(2,1)} %pre_k.1, bf16[2,16,1024]{2,1,0:T(8,128)(2,1)} %pre_v.1, ...), custom_call_target="tpu_custom_call" | custom-call | tf_op jit(solution)/shard_map/pallas_call | solution.py:1062
  211.0 2.9 %shard_map.184 = (bf16[1,512,1024]{2,1,0:T(8,128)(2,1)}, f32[1,512,1024]{2,1,0:T(8,128)}, f32[2,16,1024]{2,1,0:T(8,128)}, f32[2,16,1024]{2,1,0:T(8,128)}) custom-call(bf16[2,512,1024]{2,1,0:T(8,128)(2,1)} %get-tuple-element.6.low, f32[2,2,16,1024]{3,2,1,0:T(8,128)} %get-tuple-element.7.grads), custom_call_target="tpu_custom_call" | custom-call | tf_op jit(solution)/shard_map/pallas_call | solution.py:1080
